TPU v7x, 128 devices: a whole 4x4x4 slice. The times are simulated.
128 devices in a mesh: frames: 8 (over y_hi, x), rows: 16 (over y_lo, z, core).
Axes of the slice: x: 4, y: 4 (y_hi: 2, y_lo: 2; y = y_hi * 2 + y_lo), z: 4, core: 2. Of those that a mesh axis runs over, the one named last changes fastest.
Arguments:
- video: bfloat16 [32, 32, 32, 192], P('frames', 'rows'), may hold values from -6 to 6
- w_conv_in: bfloat16 [3, 3, 3, 192, 384], replicated, may hold values from -0.078125 to 0.078125
- w_conv_out: bfloat16 [3, 3, 3, 384, 384], replicated, may hold values from -0.0625 to 0.0625
- w_shortcut: bfloat16 [192, 384], replicated, may hold values from -0.4375 to 0.4375
- w_embed: bfloat16 [1536, 5120], P(None, 'rows'), may hold values from -0.15625 to 0.15625
- w_qkv: bfloat16 [5120, 15360], P(None, 'rows'), may hold values from -0.078125 to 0.078125
Outputs:
- projected: bfloat16 [32, 16, 16, 15360], P('frames', None, None, 'rows')
All inputs are finite; a program needn't handle non-finite values.
Results may differ from a plain program's by a relative error of at most 0.009.
Values may be sent and summed in bfloat16 or wider, within the bound.
No kernel may reach another device: no remote copies, remote signals or barrier semaphores. Data moves between devices by JAX's collectives and lax.ppermute only.
A program may use at most 384 MiB of HBM per device.

v0:
```python
import jax
import jax.numpy as jnp
from jax import lax
from jax.sharding import PartitionSpec as P


def shifted(x, axis, by):
    length = lax.axis_size(axis)
    pairs = [(i, i + by) for i in range(length) if 0 <= i + by < length]
    return lax.ppermute(x, axis, pairs)


def with_halo(cells, sides, width):
    for axis, dim in sides:
        count = lax.axis_size(axis)
        ends = count - 1
        head = lax.slice_in_dim(cells, 0, width, axis=dim)
        tail = lax.slice_in_dim(cells, cells.shape[dim] - width, cells.shape[dim], axis=dim)
        cells = jnp.concatenate(
            [
                lax.ppermute(tail, axis, [(i, (i + 1) % count) for i in range(ends)]),
                cells,
                lax.ppermute(head, axis, [((i + 1) % count, i) for i in range(ends)]),
            ],
            axis=dim,
        )
    return cells


def activate(values):
    widened = values.astype(jnp.float32)
    scaled = widened * lax.rsqrt(jnp.mean(widened * widened, axis=-1, keepdims=True) + 1e-06)
    return jax.nn.silu(scaled).astype(jnp.bfloat16)


def pad_columns(values):
    return jnp.pad(values, ((0, 0), (0, 0), (1, 1), (0, 0)))


def convolve(padded, kernel, out_frames, out_rows, out_cols):
    summed = jnp.zeros((out_frames, out_rows, out_cols, kernel.shape[-1]), jnp.float32)
    for frame_lag in range(3):
        for row_lag in range(3):
            for col_lag in range(3):
                window = padded[
                    frame_lag : frame_lag + out_frames,
                    row_lag : row_lag + out_rows,
                    col_lag : col_lag + out_cols,
                ]
                summed = summed + jnp.einsum(
                    "fhwc,cd->fhwd",
                    window,
                    kernel[frame_lag, row_lag, col_lag],
                    preferred_element_type=jnp.float32,
                )
    return summed


def shards(video, w_conv_in, w_conv_out, w_shortcut, w_embed, w_qkv):
    frame_count, row_count, col_count = (video.shape[0], video.shape[1], video.shape[2])
    first = activate(video)
    earlier = shifted(first[frame_count - 2 :], "frames", 1)
    haloed = with_halo(jnp.concatenate([earlier, first], axis=0), (("rows", 1),), 1)
    second = activate(convolve(pad_columns(haloed), w_conv_in, frame_count, row_count, col_count))
    previous = shifted(second[frame_count - 2 :], "frames", 1)
    second_haloed = with_halo(jnp.concatenate([previous, second], axis=0), (("rows", 1),), 1)
    second_padded = pad_columns(second_haloed)
    shortcut = jnp.einsum("fhwc,cd->fhwd", video, w_shortcut, preferred_element_type=jnp.float32)
    sectioned = (
        convolve(second_padded, w_conv_out, frame_count, row_count, col_count) + shortcut
    ).astype(jnp.bfloat16)
    channels = sectioned.shape[3]
    patches = sectioned.reshape(frame_count, row_count // 2, 2, col_count // 2, 2, channels)
    patches = patches.transpose(0, 1, 3, 2, 4, 5).reshape(
        frame_count, row_count // 2, col_count // 2, 4 * channels
    )
    embedded = jnp.einsum(
        "fhwc,cd->fhwd",
        lax.all_gather(patches, "rows", axis=1, tiled=True),
        w_embed,
        preferred_element_type=jnp.float32,
    ).astype(jnp.bfloat16)
    embedded = lax.all_gather(embedded, "rows", axis=3, tiled=True)
    widened = embedded.astype(jnp.float32)
    centred = widened - jnp.mean(widened, axis=-1, keepdims=True)
    normed = (
        centred * lax.rsqrt(jnp.mean(centred * centred, axis=-1, keepdims=True) + 1e-06)
    ).astype(jnp.bfloat16)
    projected = jnp.einsum("fhwd,de->fhwe", normed, w_qkv, preferred_element_type=jnp.float32)
    return projected.astype(jnp.bfloat16)


def solution(mesh):
    placed = (P("frames", "rows", None, None), P(), P(), P(), P(None, "rows"), P(None, "rows"))
    return jax.shard_map(
        shards,
        mesh=mesh,
        in_specs=placed,
        out_specs=P("frames", None, None, "rows"),
        check_vma=False,
    )
```

profile of v0, /device:TPU:1, one launch (start us, length us, event | category | flops | bytes accessed | tf_op | source)
XLA Modules:
  0.0 778.0 jit_solution(7878540350264303049)
XLA Ops:
  6.5 1.2 fusion.122
  7.7 1.2 fusion.121
  9.0 3.9 collective-permute-start
  12.9 1.3 collective-permute-done
  14.3 5.0 collective-permute-start.1
  19.2 1.9 collective-permute-start.2
  21.2 4.0 collective-permute-done.2
  25.4 1.1 fusion.150
  26.5 1.1 fusion.152
  27.6 1.1 fusion.155
  28.8 1.1 fusion.157
  29.9 1.1 fusion.160
  31.0 1.1 fusion.162
  32.2 1.1 fusion.165
  33.3 1.1 fusion.167
  34.4 1.1 fusion.170
  37.4 0.2 fusion.29
  37.8 0.2 fusion.33
  38.1 0.2 fusion.28
  38.3 0.2 fusion.35
  38.5 0.2 fusion.37
  39.5 0.3 multiply_reduce_fusion
  40.0 4.1 collective-permute-start.3
  44.1 1.6 collective-permute-done.3
  45.8 2.7 collective-permute-start.4
  48.5 1.9 collective-permute-start.5
  50.5 4.4 collective-permute-done.5
  54.9 0.3 select_maximum_fusion
  55.3 0.3 fusion.56
  55.5 0.3 fusion.58
  55.8 0.3 fusion.61
  56.1 0.3 fusion.63
  56.4 0.3 fusion.66
  56.6 0.3 fusion.68
  56.9 0.3 fusion.71
  57.2 0.3 fusion.73
  57.5 0.3 fusion.76
  57.7 0.3 fusion.78
  58.0 0.3 fusion.81
  58.3 0.3 fusion.83
  58.5 0.3 fusion.50
  58.8 0.3 fusion.88
  59.1 0.3 convolution_add_fusion.26
  59.4 0.3 convolution_add_fusion.25
  59.6 0.3 convolution_add_fusion.24
  59.9 0.3 fusion.16
  60.2 0.3 fusion.18
  60.5 0.3 fusion.20
  60.8 0.3 fusion.22
  61.1 0.3 fusion.24
  61.4 0.3 fusion.26
  61.7 0.3 convolution_add_fusion.23
  62.0 0.3 convolution_add_fusion.22
  62.2 0.3 convolution_add_fusion.21
  62.5 0.3 fusion.27
  63.3 0.8 reshape.35
  64.1 46.4 %all-gather.3.cloned.1.call-done = bf16[4,16,16,1536]{3,2,1,0:T(8,128)(2,1)} async-done(((bf16[4,1,16,1536]{3,2,1,0:T(8,128)(2,1)}), bf16[4,16,16,1536]{3,2,1,0:T(8,128)(2,1)}) %all-gather.3.cloned.1.call-update) | async-done | bytes 3145744 | tf_op jit(solution)/shard_map/all_gather | solution.py:79
  110.6 3.7 convolution_convert_fusion
  114.3 6.2 copy.9
  120.5 407.8 %all-gather.5.cloned.1.call-done = bf16[4,16,16,5120]{2,1,0,3:T(8,128)(2,1)} async-done(((bf16[4,16,16,320]{2,1,0,3:T(8,128)(2,1)}), bf16[4,16,16,5120]{2,1,0,3:T(8,128)(2,1)}) %all-gather.5.cloned.1.call-update) | async-done | bytes 10485776 | tf_op jit(solution)/shard_map/all_gather | solution.py:83
  528.2 45.2 %convert_reduce_fusion = f32[4,16,16]{2,1,0:T(8,128)S(1)} fusion(bf16[4,16,16,5120]{2,1,0,3:T(8,128)(2,1)} %all-gather.5.cloned.1.call-done), kind=kLoop, calls=%fused_computation.1 | loop fusion | flops 10484736 | bytes 10489856 | tf_op jit(solution)/shard_map/reduce_sum | solution.py:85
  573.4 45.3 %fusion.2 = f32[4,16,16]{2,1,0:T(8,128)S(1)} fusion(bf16[4,16,16,5120]{2,1,0,3:T(8,128)(2,1)} %all-gather.5.cloned.1.call-done, f32[4,16,16]{2,1,0:T(8,128)S(1)} %broadcast_multiply_fusion), kind=kLoop, calls=%fused_computation.4 | loop fusion | flops 20970496 | bytes 10493952 | tf_op jit(solution)/shard_map/reduce_sum | solution.py:87
  618.8 55.6 %fusion.3 = bf16[4,16,16,5120]{2,1,0,3:T(8,128)(2,1)} fusion(bf16[4,16,16,5120]{2,1,0,3:T(8,128)(2,1)} %all-gather.5.cloned.1.call-done, f32[4,16,16]{2,1,0:T(8,128)S(1)} %add_rsqrt_fusion, f32[4,16,16]{2,1,0:T(8,128)S(1)} %broadcast_multiply_fusion), kind=kLoop, calls=%fused_computation.5 | loop fusion | flops 20971520 | bytes 20979712 | tf_op jit(solution)/shard_map/convert_element_type | solution.py:88
  674.4 96.7 %fusion.7 = bf16[4,16,16,960]{3,2,1,0:T(8,128)(2,1)} fusion(bf16[5120,960]{0,1:T(8,128)(2,1)} %param.11, bf16[4,16,16,5120]{2,1,0,3:T(8,128)(2,1)} %fusion.3), kind=kOutput, calls=%fused_computation.11 | convolution fusion | flops 10067312640 | bytes 22282240 | tf_op jit(solution)/shard_map/fhwd,de->fhwe/dot_general | solution.py:89
  (44 shorter events, 3.8 us)
Async XLA Ops:
  6.5 104.0 %copy-start = (bf16[1536,320]{0,1:T(8,128)(2,1)S(1)}, bf16[1536,320]{0,1:T(8,128)(2,1)}, u32[]{:S(2)}) copy-start(bf16[1536,320]{0,1:T(8,128)(2,1)} %param.10) | copy-start | bytes 2949124
  6.5 104.0 %all-gather.3.cloned.1.call-start = ((), (), s32[]{:S(2)}) async-start(), calls=%async_computation | async-start | bytes 3342336 | tf_op jit(solution)/shard_map/all_gather | solution.py:79
  6.5 29.0 %copy-start.1 = (bf16[3,3,3,192,384]{4,3,2,1,0:T(8,128)(2,1)S(1)}, bf16[3,3,3,192,384]{4,3,2,1,0:T(8,128)(2,1)}, u32[]{:S(2)}) copy-start(bf16[3,3,3,192,384]{4,3,2,1,0:T(8,128)(2,1)} %param.7) | copy-start | bytes 11943940
  9.0 5.3 collective-permute-start
  14.3 6.9 collective-permute-start.1
  19.2 5.9 collective-permute-start.2
  37.8 17.4 %slice-start = ((s8[7962624]{0:T(1024)(128)(4,1)}), s8[4194304]{0:T(1024)(128)(4,1)S(1)}, s32[]{:S(2)}) async-start(s8[7962624]{0:T(1024)(128)(4,1)} %bitcast.406), calls=%async_computation.2 | async-start | bytes 8388608
  38.5 16.7 %slice-start.1 = ((s8[7962624]{0:T(1024)(128)(4,1)}), s8[3768320]{0:T(1024)(128)(4,1)S(1)}, s32[]{:S(2)}) async-start(s8[7962624]{0:T(1024)(128)(4,1)} %bitcast.406), calls=%async_computation.3 | async-start | bytes 7536640
  40.0 5.7 collective-permute-start.3
  45.8 4.8 collective-permute-start.4
  48.5 6.5 collective-permute-start.5
  60.5 2.3 copy-start.2
  60.5 2.3 copy-start.3
  64.1 464.1 %all-gather.5.cloned.1.call-start = ((), (), s32[]{:S(2)}) async-start(), calls=%async_computation.1 | async-start | bytes 89128960 | tf_op jit(solution)/shard_map/all_gather | solution.py:83
Sparse Core Ops, SparseCore 0:
  64.2 46.3 all-gather.2
  120.6 407.6 all-gather.4
where the time goes:
time: 778 us
  waiting for transfers between devices  466 us (60%)
  other arithmetic  149 us (19%)
  matrix products  122 us (16%)
  starting transfers between devices  19.6 us (3%)
  between operations  14 us (2%)
    all_gather x1, waiting for transfers between devices, shards(): embedded = lax.all_gather(embedded, 'rows', axis=3, tiled=True)  408 us
    dot_general x1, matrix products, shards(): jnp.einsum('fhwd,de->fhwe', normed, w_qkv, preferred_element_type=jnp.flo...  96.7 us
    convert_element_type x1, other arithmetic, shards(): normed = (centred * lax.rsqrt(jnp.mean(centred * centred, axis=-1, keepdi...  55.6 us
    all_gather x1, waiting for transfers between devices, shards(): lax.all_gather(patches, 'rows', axis=1, tiled=True)  46.4 us
    reduce_sum x1, other arithmetic, shards(): jnp.mean(centred * centred, axis=-1, keepdims=True) + 1e-06  45.3 us
    reduce_sum x1, other arithmetic, shards(): centred = widened - jnp.mean(widened, axis=-1, keepdims=True)  45.2 us
    dot_general x54, matrix products, convolve(): jnp.einsum('fhwc,cd->fhwd', window, kernel[frame_lag, row_lag, col_lag],...  21.5 us
  transfers between devices with their start and end apart: 8, of which 7 were waited for; matrix products, arithmetic and copies ran while one was open for 0% of the time, Pallas kernels for 0%

commit v1 on v0

v1 whole, which is shorter than its diff:
```python
import jax
import jax.numpy as jnp
from jax import lax
from jax.experimental import pallas as pl
from jax.experimental.pallas import tpu as pltpu
from jax.sharding import PartitionSpec as P

F32 = jnp.float32
BF16 = jnp.bfloat16
MIB = 1 << 20

FRAMES_PAIRS = 8
ROWS_PAIRS = 16


def along_x(by):
    return [(i, i // 4 * 4 + (i + by) % 4) for i in range(FRAMES_PAIRS)]


SWAP_Y_HI = [(i, i ^ 4) for i in range(FRAMES_PAIRS)]
NEXT_FRAMES = [(i, (i + 1) % FRAMES_PAIRS) for i in range(FRAMES_PAIRS)]


def along_z(by):
    return [(i, i // 8 * 8 + (i + 2 * by) % 8) for i in range(ROWS_PAIRS)]


SWAP_Y_LO = [(i, i ^ 8) for i in range(ROWS_PAIRS)]
SWAP_CORE = [(i, i ^ 1) for i in range(ROWS_PAIRS)]
SWAP_CHIP = [(i, (i + 1) % ROWS_PAIRS if i % 2 else (i - 1) % ROWS_PAIRS) for i in range(ROWS_PAIRS)]


def by_rows(x, pairs):
    return lax.ppermute(x, "rows", pairs)


def by_frames(x, pairs):
    return lax.ppermute(x, "frames", pairs)


def whole(memory=pltpu.VMEM):
    return pl.BlockSpec(memory_space=memory)


def normalized_silu(v):
    u = v * lax.rsqrt(jnp.mean(v * v, axis=-1, keepdims=True) + 1e-06)
    return u / (1.0 + jnp.exp(-u))


def three_columns(v):
    col = lax.broadcasted_iota(jnp.int32, v.shape, 0) % 32
    n = v.shape[0]
    before = jnp.where(col == 0, 0.0, pltpu.roll(v, 1, 0))
    after = jnp.where(col == 31, 0.0, pltpu.roll(v, n - 1, 0))
    return [before.astype(BF16), v.astype(BF16), after.astype(BF16)]


def conv_kernel(
    place, own, side_core, side_chip, back, back_core, back_chip, w_in, w_out, w_short, out, first, second, vin, vout, flat, sems
):
    core, at_first_frames, at_first_rows, at_last_rows = (place[0], place[1], place[2], place[3])
    for k in range(9):
        pltpu.make_async_copy(w_in.at[k], vin.at[k], sems.at[k]).start()
    for k in range(9):
        pltpu.make_async_copy(w_out.at[k], vout.at[k], sems.at[9 + k]).start()

    core_row = jnp.where(core == 0, 4, 0)
    chip_row = 4 - core_row
    for frame, blocks in ((0, (back, back_core, back_chip)), (4, (own, side_core, side_chip))):
        for ref, row in zip(blocks, (2, core_row, chip_row)):
            v = normalized_silu(ref[...].astype(F32).reshape(256, 192))
            if frame == 0:
                v = jnp.where(at_first_frames == 1, 0.0, v)
            if ref is not back and ref is not own:
                outside = jnp.where(row == 0, at_first_rows, at_last_rows)
                v = jnp.where(outside == 1, 0.0, v)
            cols = jnp.concatenate(three_columns(v), axis=1)
            first[pl.ds(frame, 4), pl.ds(row, 2)] = cols.reshape(4, 2, 32, 576)

    acc = None
    for t in range(3):
        for i in range(3):
            k = 3 * t + i
            pltpu.make_async_copy(w_in.at[k], vin.at[k], sems.at[k]).wait()
            term = jnp.dot(first[t : t + 6, i : i + 4].reshape(768, 576), vin[k], preferred_element_type=F32)
            acc = term if acc is None else acc + term
    acc = normalized_silu(acc)
    line = lax.broadcasted_iota(jnp.int32, acc.shape, 0) // 32
    row, frame = line % 4, line // 4
    outside = (
        ((at_first_frames == 1) & (frame < 2))
        | ((at_first_rows == 1) & (row == 0))
        | ((at_last_rows == 1) & (row == 3))
    )
    acc = jnp.where(outside, 0.0, acc)
    for j, cols in enumerate(three_columns(acc)):
        second[:, :, :, 384 * j : 384 * (j + 1)] = cols.reshape(6, 4, 32, 384)

    acc = jnp.dot(own[...].reshape(256, 192), w_short[...], preferred_element_type=F32)
    for t in range(3):
        for i in range(3):
            k = 3 * t + i
            pltpu.make_async_copy(w_out.at[k], vout.at[k], sems.at[9 + k]).wait()
            acc += jnp.dot(second[t : t + 4, i : i + 2].reshape(256, 1152), vout[k], preferred_element_type=F32)
    for n in range(3):
        flat[n] = acc[:, 128 * n : 128 * (n + 1)].reshape(8, 32, 128)
    for f in range(4):
        for a in range(2):
            for b in range(2):
                for n in range(3):
                    part = 384 * (2 * a + b) + 128 * n
                    cols = flat[n, 2 * f + a, pl.ds(b, 16, stride=2), :]
                    out[16 * f : 16 * (f + 1), part : part + 128] = cols.astype(BF16)


def convolutions(place, blocks, w_in, w_out, w_short):
    return pl.pallas_call(
        conv_kernel,
        out_shape=jax.ShapeDtypeStruct((64, 1536), BF16),
        in_specs=[whole(pltpu.SMEM)] + [whole()] * 6 + [whole(pl.ANY)] * 2 + [whole()],
        out_specs=whole(),
        scratch_shapes=[
            pltpu.VMEM((8, 6, 32, 576), BF16),
            pltpu.VMEM((6, 4, 32, 1152), BF16),
            pltpu.VMEM((9, 576, 384), BF16),
            pltpu.VMEM((9, 1152, 384), BF16),
            pltpu.VMEM((3, 8, 32, 128), F32),
            pltpu.SemaphoreType.DMA((18,)),
        ],
        compiler_params=pltpu.CompilerParams(vmem_limit_bytes=40 * MIB),
        cost_estimate=pl.CostEstimate(flops=5 * 10**9, bytes_accessed=13 * 10**6, transcendentals=10**6),
        name="convolutions",
    )(place, *blocks, w_in.reshape(9, 576, 384), w_out.reshape(9, 1152, 384), w_short)


def fold_kernel(chips, core, same, other, w_qkv, out, acc, sums):
    step = pl.program_id(0)
    ones = jnp.ones((16, 320), BF16)
    total, row = None, None
    for ref, place in ((same, core[0]), (other, 1 - core[0])):
        block = ref[0]
        rows = pl.ds(pl.multiple_of(place * 320, 320), 320)
        term = jnp.dot(jnp.concatenate([block, ones], axis=0), w_qkv[rows, :], preferred_element_type=F32)
        part = jnp.sum(block.astype(F32), axis=1, keepdims=True)
        total = term if total is None else total + term
        row = part if row is None else row + part
    row = jnp.broadcast_to(row, (192, 128))

    @pl.when(step == 0)
    def _():
        acc[...] = total
        sums[...] = row

    @pl.when(step > 0)
    def _():
        acc[...] += total
        sums[...] += row

    @pl.when(step == pl.num_programs(0) - 1)
    def _():
        mean = sums[:, :1] * (1.0 / 5120)
        out[...] = (acc[:192] - mean * acc[192:193]).astype(BF16)


def fold(chips, core, same, other, w_qkv):
    grid = pltpu.PrefetchScalarGridSpec(
        num_scalar_prefetch=2,
        grid=(8,),
        in_specs=[
            pl.BlockSpec((1, 192, 320), lambda s, chips, core: (s, 0, 0)),
            pl.BlockSpec((1, 192, 320), lambda s, chips, core: (s, 0, 0)),
            pl.BlockSpec((640, 960), lambda s, chips, core: (chips[s], 0)),
        ],
        out_specs=pl.BlockSpec((192, 960), lambda s, chips, core: (0, 0)),
        scratch_shapes=[pltpu.VMEM((208, 960), F32), pltpu.VMEM((192, 128), F32)],
    )
    return pl.pallas_call(
        fold_kernel,
        out_shape=jax.ShapeDtypeStruct((192, 960), BF16),
        grid_spec=grid,
        compiler_params=pltpu.CompilerParams(vmem_limit_bytes=32 * MIB),
        cost_estimate=pl.CostEstimate(flops=3 * 10**9, bytes_accessed=12 * 10**6, transcendentals=0),
        name="fold",
    )(chips, core, same, other, w_qkv)


def place_blocks(rows_at, pieces, target, sems):
    copies, block = [], 0
    for n, piece in enumerate(pieces):
        for k in range(piece.shape[0] // 64):
            copies.append(
                pltpu.make_async_copy(piece.at[pl.ds(64 * k, 64)], target.at[rows_at[block]], sems.at[block])
            )
            block += 1
    return copies


def moments_kernel(count, rows_at, *refs):
    pieces, w_embed, out, tokens, sems = (refs[:count], refs[count], refs[count + 1], refs[count + 2], refs[count + 3])
    copies = place_blocks(rows_at, pieces, tokens, sems)
    for copy in copies:
        copy.start()
    for copy in copies:
        copy.wait()
    lane = lax.broadcasted_iota(jnp.int32, (256, 128), 1)
    for g in range(4):
        e = jnp.dot(tokens[4 * g : 4 * g + 4].reshape(256, 1536), w_embed[...], preferred_element_type=F32)
        mean = jnp.mean(e, axis=1, keepdims=True)
        spread = jnp.sum((e - mean) * (e - mean), axis=1, keepdims=True)
        turned = jnp.where(lane == 0, mean, spread).T
        out[g : g + 1, :] = turned[0:1, :]
        out[4 + g : 5 + g, :] = turned[1:2, :]


def moments(rows_at, pieces, w_embed):
    count = len(pieces)
    return pl.pallas_call(
        lambda *refs: moments_kernel(count, *refs),
        out_shape=jax.ShapeDtypeStruct((8, 256), F32),
        in_specs=[whole(pltpu.SMEM)] + [whole(pl.ANY)] * count + [whole()],
        out_specs=whole(),
        scratch_shapes=[pltpu.VMEM((16, 64, 1536), BF16), pltpu.SemaphoreType.DMA((16,))],
        compiler_params=pltpu.CompilerParams(vmem_limit_bytes=32 * MIB),
        cost_estimate=pl.CostEstimate(flops=10**9, bytes_accessed=5 * 10**6, transcendentals=0),
        name="moments",
    )(rows_at, *pieces, w_embed)


def merged(parts, features):
    mean = sum(part[:4] for part in parts) * (1.0 / len(parts))
    spread = sum(part[4:] for part in parts)
    spread = spread + features * sum((part[:4] - mean) * (part[:4] - mean) for part in parts)
    return jnp.concatenate([mean, spread], axis=0)


def project_kernel(count, layout, rows_at, fold_at, *refs):
    pieces, refs = refs[:count], refs[count:]
    weights, refs = refs[: len(layout)], refs[len(layout) :]
    stats, out, tokens, folded, sems, fold_sems = refs
    copies = place_blocks(rows_at, pieces, tokens, sems)
    for n, (ref, (source, size, at, inside)) in enumerate(zip(weights, layout)):
        start = pl.multiple_of(fold_at[at] * 192 + inside, 96)
        copies.append(
            pltpu.make_async_copy(ref.at[pl.ds(source, size)], folded.at[pl.ds(start, size)], fold_sems.at[n])
        )
    for copy in copies:
        copy.start()
    for copy in copies:
        copy.wait()
    for g in range(4):
        acc = jnp.dot(tokens[4 * g : 4 * g + 4].reshape(256, 1536), folded[...], preferred_element_type=F32)
        scale = lax.rsqrt(stats[4 + g : 5 + g, :] * (1.0 / 5120) + 1e-06)
        scale = jnp.broadcast_to(scale, (128, 256)).T[:, :1]
        result = (acc * scale).astype(BF16).reshape(4, 4, 16, 960)
        for r in range(4):
            out[:, 4 * g + r] = result[r]


def project(rows_at, fold_at, pieces, weights, layout, stats):
    count = len(pieces)
    return pl.pallas_call(
        lambda *refs: project_kernel(count, layout, *refs),
        out_shape=jax.ShapeDtypeStruct((4, 16, 16, 960), BF16),
        in_specs=[whole(pltpu.SMEM)] * 2 + [whole(pl.ANY)] * (count + len(weights)) + [whole()],
        out_specs=whole(),
        scratch_shapes=[
            pltpu.VMEM((16, 64, 1536), BF16),
            pltpu.VMEM((1536, 960), BF16),
            pltpu.SemaphoreType.DMA((16,)),
            pltpu.SemaphoreType.DMA((len(weights),)),
        ],
        compiler_params=pltpu.CompilerParams(vmem_limit_bytes=40 * MIB),
        cost_estimate=pl.CostEstimate(flops=3 * 10**9, bytes_accessed=8 * 10**6, transcendentals=0),
        name="project",
    )(rows_at, fold_at, *pieces, *weights, stats)


def shards(video, w_conv_in, w_conv_out, w_shortcut, w_embed, w_qkv):
    f, r = lax.axis_index("frames"), lax.axis_index("rows")
    y_hi, x = f // 4, f % 4
    y_lo, z, core = r // 8, r // 2 % 4, r % 2

    mine = lax.dynamic_slice_in_dim(w_embed, f * 192, 192, axis=0)
    near = jnp.stack([mine, by_rows(mine, SWAP_Y_LO)])
    same = jnp.concatenate([near] + [by_rows(near, along_z(by)) for by in (1, -1, 2)])
    other = by_rows(same, SWAP_CORE)
    chips = jnp.stack([(y_lo ^ b) * 4 + (z - by) % 4 for by in (0, 1, -1, 2) for b in (0, 1)]).astype(jnp.int32)
    folded = fold(chips, core.astype(jnp.int32).reshape(1), same, other, w_qkv)

    from_left, from_right = by_frames(folded, along_x(1)), by_frames(folded, along_x(-1))
    across = by_frames(folded, SWAP_Y_HI)
    far_left = by_frames(jnp.concatenate([from_left[:96], across]), along_x(1))
    far_right = by_frames(jnp.concatenate([from_right[96:], across]), along_x(-1))
    last_left = by_frames(far_left[96:192], along_x(1))
    last_right = by_frames(far_right[192:], along_x(-1))
    weights = [folded, from_left, from_right, across, far_left, far_left, far_right, far_right, last_left, last_right]
    layout = [
        (0, 192, 0, 0),
        (0, 192, 1, 0),
        (0, 192, 2, 0),
        (0, 192, 4, 0),
        (0, 96, 3, 0),
        (96, 192, 5, 0),
        (0, 96, 3, 96),
        (96, 192, 6, 0),
        (0, 96, 7, 0),
        (0, 96, 7, 96),
    ]
    fold_at = jnp.stack([(y_hi ^ h) * 4 + (x + by) % 4 for h in (0, 1) for by in (0, -1, 1, 2)]).astype(jnp.int32)

    back = by_frames(video, NEXT_FRAMES)
    side_core, side_chip = by_rows(video, SWAP_CORE), by_rows(video, SWAP_CHIP)
    back_core, back_chip = by_rows(back, SWAP_CORE), by_rows(back, SWAP_CHIP)
    place = jnp.stack([core, f == 0, r == 0, r == 15]).astype(jnp.int32)
    patches = convolutions(
        place, (video, side_core, side_chip, back, back_core, back_chip), w_conv_in, w_conv_out, w_shortcut
    )

    near = jnp.concatenate([patches, by_rows(patches, SWAP_Y_LO)])
    from_low, from_high = by_rows(near, along_z(1)), by_rows(near, along_z(-1))
    far_low = by_rows(from_low[:64], along_z(1))
    far_high = by_rows(from_high[64:], along_z(-1))
    most = jnp.concatenate([near, from_low, from_high])
    rest = jnp.concatenate([far_low, far_high])
    pieces = [most, rest, by_rows(most, SWAP_CORE), by_rows(rest, SWAP_CORE)]
    rows_at = jnp.stack(
        [
            ((y_lo ^ b) * 4 + (z + by) % 4) * 2 + (core ^ c)
            for c in (0, 1)
            for by in (0, -1, 1, 2)
            for b in (0, 1)
        ]
    ).astype(jnp.int32)

    stats = moments(rows_at, pieces, w_embed)
    stats = merged([stats, by_rows(stats, SWAP_Y_LO)], 320)
    stats = merged([stats] + [by_rows(stats, along_z(by)) for by in (1, -1, 2)], 640)
    stats = merged([stats, by_rows(stats, SWAP_CORE)], 2560)
    return project(rows_at, fold_at, pieces, weights, layout, stats)


def solution(mesh):
    placed = (P("frames", "rows", None, None), P(), P(), P(), P(None, "rows"), P(None, "rows"))
    return jax.shard_map(
        shards,
        mesh=mesh,
        in_specs=placed,
        out_specs=P("frames", None, None, "rows"),
        check_vma=False,
    )
```

time: 778 us -> 159 us (0.20)
  waiting for transfers between devices: 466 us -> 38.4 us
  other arithmetic: 149 us -> 3.74 us
  matrix products: 122 us -> 0 us
  Pallas kernels: 0 us -> 41.3 us
  local copies, waits for them, and re-layouts: 7.22 us -> 31.1 us
  starting transfers between devices: 19.6 us -> 41.9 us
  between operations: 14 us -> 0.4 us
    all_gather x2 -> x0, waiting for transfers between devices: 454 us -> none  [the longest x1 408 us: shards(): embedded = lax.all_gather(embedded, 'rows', axis=3, tiled=True)]
    dot_general x57 -> x0, matrix products: 122 us -> none  [the longest x1 96.7 us: shards(): jnp.einsum('fhwd,de->fhwe', normed, w_qkv, preferred_element_type=jnp.flo...]
    reduce_sum x3 -> x0, other arithmetic: 91.7 us -> none  [the longest x1 45.3 us: shards(): jnp.mean(centred * centred, axis=-1, keepdims=True) + 1e-06]
    convert_element_type x3 -> x0, other arithmetic: 57 us -> none  [the longest x1 55.6 us: shards(): normed = (centred * lax.rsqrt(jnp.mean(centred * centred, axis=-1, keepdi...]
    pallas_call x0 -> x4, Pallas kernels: none -> 41.3 us  [the longest x1 17.4 us: convolutions(): pl.pallas_call(conv_kernel, out_shape=jax.ShapeDtypeStruct((64, 1536), BF...]
    unnamed x12 -> x19, local copies, waits for them, and re-layouts: 0.04 us -> 28.4 us
    ppermute x6 -> x29, waiting for transfers between devices: 11.5 us -> 38.4 us  [the longest x8 21.8 us: by_frames(): return lax.ppermute(x, 'frames', pairs)]
    ppermute x6 -> x29, starting transfers between devices: 19.5 us -> 41.9 us  [the longest x21 33 us: by_rows(): return lax.ppermute(x, 'rows', pairs)]
  transfers between devices with their start and end apart: 8 -> 29, of which waited for: 7 -> 12; matrix products, arithmetic and copies ran while one was open for 0% -> 14% of each run, Pallas kernels for 0% -> 20%
where the time goes in v1:
time: 159 us; the launch traced here: 157 us
  starting transfers between devices  41.9 us (26%)
  Pallas kernels  41.3 us (26%)
  waiting for transfers between devices  38.4 us (24%)
  local copies, waits for them, and re-layouts  31.1 us (20%)
  other arithmetic  3.74 us (2%)
    ppermute x21, starting transfers between devices, by_rows(): return lax.ppermute(x, 'rows', pairs)  33 us
    unnamed x19, local copies, waits for them, and re-layouts  28.4 us
    ppermute x8, waiting for transfers between devices, by_frames(): return lax.ppermute(x, 'frames', pairs)  21.8 us
    pallas_call x1, Pallas kernels, convolutions(): pl.pallas_call(conv_kernel, out_shape=jax.ShapeDtypeStruct((64, 1536), BF...  17.4 us
    ppermute x21, waiting for transfers between devices, by_rows(): return lax.ppermute(x, 'rows', pairs)  16.6 us
    pallas_call x1, Pallas kernels, project(): pl.pallas_call(lambda *refs: project_kernel(count, layout, *refs), out_sh...  9.43 us
    ppermute x8, starting transfers between devices, by_frames(): return lax.ppermute(x, 'frames', pairs)  8.92 us
    pallas_call x1, Pallas kernels, fold(): pl.pallas_call(fold_kernel, out_shape=jax.ShapeDtypeStruct((192, 960), BF...  8.64 us
  transfers between devices with their start and end apart: 29, of which 12 were waited for; matrix products, arithmetic and copies ran while one was open for 14% of the time, Pallas kernels for 20%

profile of v1, /device:TPU:1, one launch (start us, length us, event | category | flops | bytes accessed | tf_op | source)
XLA Modules:
  0.0 156.8 jit_solution(15770823088644440111)
XLA Ops:
  0.0 1.7 %copy.7.refs_5_ = bf16[1536,320]{1,0:T(8,128)(2,1)S(1)} copy(bf16[1536,320]{0,1:T(8,128)(2,1)} %param.10) | data formatting | bytes 1966080 | tf_op args[4]
  1.7 0.7 constant_dynamic-update-slice_fusion.6
  2.4 2.1 %collective-permute-start.12 = (bf16[192,320]{1,0:T(8,128)(2,1)}, bf16[192,320]{1,0:T(8,128)(2,1)S(1)}, u32[]{:S(2)}, u32[]{:S(2)}) collective-permute-start(bf16[192,320]{1,0:T(8,128)(2,1)} %get-tuple-element.10), channel_id=1, source_target_pairs={{0,8},{1,9},{2,10},{3,11},{4,12},{5,13},{6,14},{7,15},{8,0},{9,1},... | collective-permute-start | bytes 368648 | tf_op jit(solution)/shard_map/ppermute | solution.py:34
  4.5 2.5 %collective-permute-start.1 = (bf16[4,2,32,192]{3,2,1,0:T(8,128)(2,1)S(1)}, bf16[4,2,32,192]{3,2,1,0:T(8,128)(2,1)S(1)}, u32[]{:S(2)}, u32[]{:S(2)}) collective-permute-start(bf16[4,2,32,192]{3,2,1,0:T(8,128)(2,1)S(1)} %copy-done.4), channel_id=1, source_target_pairs={{0,15},{1,2},{2,1},{3,4},{4,3},{5,6},{6,5},{7,8},{8,7},{9,10},{10,... | collective-permute-start | bytes 294920 | tf_op jit(solution)/shard_map/ppermute | solution.py:34
  7.0 1.6 collective-permute-start
  8.6 1.2 collective-permute-start.2
  9.8 0.1 pad_add_fusion.place
  9.9 7.5 %collective-permute-done.2.back = bf16[4,2,32,192]{3,2,1,0:T(8,128)(2,1)S(1)} collective-permute-done((bf16[4,2,32,192]{3,2,1,0:T(8,128)(2,1)S(1)}, bf16[4,2,32,192]{3,2,1,0:T(8,128)(2,1)S(1)}, u32[]{:S(2)}, u32[]{:S(2)}) %collective-permute-start.2) | collective-permute-done | bytes 98336 | tf_op jit(solution)/shard_map/ppermute | solution.py:38
  17.4 0.7 collective-permute-start.4
  18.1 0.1 collective-permute-start.3
  18.2 1.0 pad_maximum_fusion.4
  19.1 1.9 %collective-permute-start.15 = (bf16[2,192,320]{2,1,0:T(8,128)(2,1)S(1)}, bf16[2,192,320]{2,1,0:T(8,128)(2,1)S(1)}, u32[]{:S(2)}, u32[]{:S(2)}) collective-permute-start(bf16[2,192,320]{2,1,0:T(8,128)(2,1)S(1)} %pad_maximum_fusion.4), channel_id=1, source_target_pairs={{0,4},{1,5},{2,6},{3,7},{4,0},{5,1},{6,2},{7,3},{8,12},{9,13},{10,... | collective-permute-start | bytes 737288 | tf_op jit(solution)/shard_map/ppermute | solution.py:34
  21.0 0.0 collective-permute-done.1.side_chip
  21.0 1.9 %collective-permute-start.14 = (bf16[2,192,320]{2,1,0:T(8,128)(2,1)S(1)}, bf16[2,192,320]{2,1,0:T(8,128)(2,1)S(1)}, u32[]{:S(2)}, u32[]{:S(2)}) collective-permute-start(bf16[2,192,320]{2,1,0:T(8,128)(2,1)S(1)} %pad_maximum_fusion.4), channel_id=1, source_target_pairs={{0,6},{1,7},{2,0},{3,1},{4,2},{5,3},{6,4},{7,5},{8,14},{9,15},{10,... | collective-permute-start | bytes 737288 | tf_op jit(solution)/shard_map/ppermute | solution.py:34
  22.9 0.7 collective-permute-start.13
  23.6 0.0 copy-start.1
  23.6 3.3 %copy-done.1 = bf16[3,3,3,384,384]{4,3,2,1,0:T(8,128)(2,1)S(1)} copy-done((bf16[3,3,3,384,384]{4,3,2,1,0:T(8,128)(2,1)S(1)}, bf16[3,3,3,384,384]{4,3,2,1,0:T(8,128)(2,1)}, u32[]{:S(2)}) %copy-start.1) | copy-done | bytes 7962648
  26.9 2.1 %copy-done.2 = bf16[3,3,3,192,384]{4,3,2,1,0:T(8,128)(2,1)S(1)} copy-done((bf16[3,3,3,192,384]{4,3,2,1,0:T(8,128)(2,1)S(1)}, bf16[3,3,3,192,384]{4,3,2,1,0:T(8,128)(2,1)}, u32[]{:S(2)}) %copy-start.2) | copy-done | bytes 3981336
  29.0 17.4 %convolutions.1 = bf16[64,1536]{1,0:T(8,128)(2,1)S(1)} custom-call(s32[4]{0:T(128)S(1)} %pad_add_fusion.place, bf16[4,2,32,192]{3,2,1,0:T(8,128)(2,1)S(1)} %copy-done.4, bf16[4,2,32,192]{3,2,1,0:T(8,128)(2,1)S(1)} %collective-permute-done.side_core, bf16[4,2,32,192]{3,2,1,0:T(8,128)(2,1)S(1)} %collective-permute-done.1.side_chip, ...), custom_call_target="tpu_custom_call" | custom-call | flops 5000000000 | bytes 13000000 | tf_op jit(solution)/shard_map/convolutions/pallas_call | solution.py:117
  46.4 0.5 collective-permute-start.5
  47.0 4.0 %collective-permute-done.5 = bf16[64,1536]{1,0:T(8,128)(2,1)S(1)} collective-permute-done((bf16[64,1536]{1,0:T(8,128)(2,1)S(1)}, bf16[64,1536]{1,0:T(8,128)(2,1)S(1)}, u32[]{:S(2)}, u32[]{:S(2)}) %collective-permute-start.5) | collective-permute-done | bytes 196640 | tf_op jit(solution)/shard_map/ppermute | solution.py:34
  51.1 2.6 %collective-permute-start.7 = (bf16[128,1536]{1,0:T(8,128)(2,1)S(1)}, bf16[128,1536]{1,0:T(8,128)(2,1)S(1)}, u32[]{:S(2)}, u32[]{:S(2)}) collective-permute-start(bf16[128,1536]{1,0:T(8,128)(2,1)S(1)} %pad_maximum_fusion.3), channel_id=1, source_target_pairs={{0,6},{1,7},{2,0},{3,1},{4,2},{5,3},{6,4},{7,5},{8,14},{9,15},{10,... | collective-permute-start | bytes 1179656 | tf_op jit(solution)/shard_map/ppermute | solution.py:34
  53.8 2.9 %collective-permute-start.16 = (bf16[8,192,320]{2,1,0:T(8,128)(2,1)S(1)}, bf16[8,192,320]{2,1,0:T(8,128)(2,1)}, u32[]{:S(2)}, u32[]{:S(2)}) collective-permute-start(bf16[8,192,320]{2,1,0:T(8,128)(2,1)S(1)} %constant_dynamic-update-slice_fusion.2.same), channel_id=1, source_target_pairs={{0,1},{1,0},{2,3},{3,2},{4,5},{5,4},{6,7},{7,6},{8,9},{9,8},{10,11... | collective-permute-start | bytes 2949128 | tf_op jit(solution)/shard_map/ppermute | solution.py:34
  56.6 6.3 %collective-permute-done.6 = bf16[128,1536]{1,0:T(8,128)(2,1)S(1)} collective-permute-done((bf16[128,1536]{1,0:T(8,128)(2,1)S(1)}, bf16[128,1536]{1,0:T(8,128)(2,1)S(1)}, u32[]{:S(2)}, u32[]{:S(2)}) %collective-permute-start.6) | collective-permute-done | bytes 393248 | tf_op jit(solution)/shard_map/ppermute | solution.py:34
  62.9 0.7 slice.84
  63.6 0.1 pad_maximum_fusion.refs_1_.refs_2_
  63.7 0.7 copy-done.5
  64.3 3.5 %collective-permute-start.10 = (bf16[384,1536]{1,0:T(8,128)(2,1)S(1)}, bf16[384,1536]{1,0:T(8,128)(2,1)}, u32[]{:S(2)}, u32[]{:S(2)}) collective-permute-start(bf16[384,1536]{1,0:T(8,128)(2,1)S(1)} %pad_maximum_fusion.refs_1_.refs_2_), channel_id=1, source_target_pairs={{0,1},{1,0},{2,3},{3,2},{4,5},{5,4},{6,7},{7,6},{8,9},{9,8},{10,11... | collective-permute-start | bytes 3538952 | tf_op jit(solution)/shard_map/ppermute | solution.py:34
  67.8 14.3 %copy.8.w_qkv = bf16[5120,960]{1,0:T(8,128)(2,1)} copy(bf16[5120,960]{0,1:T(8,128)(2,1)} %param.11) | data formatting | bytes 19660800 | tf_op args[5]
  82.1 0.1 stack.180.chips
  82.2 0.9 slice.85
  83.1 3.0 %collective-permute-start.9 = (bf16[64,1536]{1,0:T(8,128)(2,1)S(1)}, bf16[64,1536]{1,0:T(8,128)(2,1)S(1)}, u32[]{:S(2)}, u32[]{:S(2)}) collective-permute-start(bf16[64,1536]{1,0:T(8,128)(2,1)S(1)} %slice.85), channel_id=1, source_target_pairs={{0,6},{1,7},{2,0},{3,1},{4,2},{5,3},{6,4},{7,5},{8,14},{9,15},{10,... | collective-permute-start | bytes 589832 | tf_op jit(solution)/shard_map/ppermute | solution.py:34
  86.1 1.6 %constant_dynamic-update-slice_fusion.1 = bf16[128,1536]{1,0:T(8,128)(2,1)} fusion(bf16[64,1536]{1,0:T(8,128)(2,1)} %collective-permute-done.8), kind=kLoop, calls=%fused_computation.6 | loop fusion | bytes 393216
  87.7 2.7 %collective-permute-done.9 = bf16[64,1536]{1,0:T(8,128)(2,1)S(1)} collective-permute-done((bf16[64,1536]{1,0:T(8,128)(2,1)S(1)}, bf16[64,1536]{1,0:T(8,128)(2,1)S(1)}, u32[]{:S(2)}, u32[]{:S(2)}) %collective-permute-start.9) | collective-permute-done | bytes 196640 | tf_op jit(solution)/shard_map/ppermute | solution.py:34
  90.5 0.7 constant_dynamic-update-slice_fusion.refs_2_.refs_3_
  91.2 0.8 collective-permute-start.11
  91.9 4.0 %copy-done = bf16[5120,960]{1,0:T(8,128)(2,1)S(1)} copy-done((bf16[5120,960]{1,0:T(8,128)(2,1)S(1)}, bf16[5120,960]{1,0:T(8,128)(2,1)}, u32[]{:S(2)}) %copy-start) | copy-done | bytes 9830424
  95.9 8.6 %fold.1.refs_6_ = bf16[192,960]{1,0:T(8,128)(2,1)} custom-call(s32[8]{0:T(128)S(1)} %stack.180.chips, s32[1]{0:T(128)} %bitcast.24.core, bf16[8,192,320]{2,1,0:T(8,128)(2,1)S(1)} %constant_dynamic-update-slice_fusion.2.same, bf16[8,192,320]{2,1,0:T(8,128)(2,1)} %collective-permute-done.16.other, bf16[5120,960]{1,0:T(8,128)(2,1)S(1)} %copy-done), custom_call_target="tpu_custom_call" | custom-call | flops 3000000000 | bytes 12000000 | tf_op jit(solution)/shard_map/fold/pallas_call | solution.py:177
  104.6 1.5 collective-permute-start.17
  106.0 2.7 %collective-permute-start.19 = (bf16[192,960]{1,0:T(8,128)(2,1)}, bf16[192,960]{1,0:T(8,128)(2,1)S(1)}, u32[]{:S(2)}, u32[]{:S(2)}) collective-permute-start(bf16[192,960]{1,0:T(8,128)(2,1)} %fold.1.refs_6_), channel_id=1, source_target_pairs={{0,64},{16,80},{32,96},{48,112},{64,0},{80,16},{96,32},{112,48},{1... | collective-permute-start | bytes 1105928 | tf_op jit(solution)/shard_map/ppermute | solution.py:38
  108.7 0.1 stack.154.refs_0_
  108.8 6.7 %collective-permute-done.18.refs_8_ = bf16[192,960]{1,0:T(8,128)(2,1)S(1)} collective-permute-done((bf16[192,960]{1,0:T(8,128)(2,1)}, bf16[192,960]{1,0:T(8,128)(2,1)S(1)}, u32[]{:S(2)}, u32[]{:S(2)}) %collective-permute-start.18) | collective-permute-done | bytes 368672 | tf_op jit(solution)/shard_map/ppermute | solution.py:38
  115.6 1.2 collective-permute-done.17.refs_7_
  116.8 5.8 %moments.1 = f32[8,256]{1,0:T(8,128)S(1)} custom-call(s32[16]{0:T(128)S(1)} %stack.154.refs_0_, bf16[384,1536]{1,0:T(8,128)(2,1)S(1)} %pad_maximum_fusion.refs_1_.refs_2_, bf16[128,1536]{1,0:T(8,128)(2,1)} %constant_dynamic-update-slice_fusion.refs_2_.refs_3_, bf16[384,1536]{1,0:T(8,128)(2,1)} %collective-permute-done.10.refs_3_.refs_4_, ...), custom_call_target="tpu_custom_call" | custom-call | flops 1000000000 | bytes 5000000 | tf_op jit(solution)/shard_map/moments/pallas_call | solution.py:217
  122.6 1.6 %collective-permute-start.24 = (f32[8,256]{1,0:T(8,128)S(1)}, f32[8,256]{1,0:T(8,128)S(1)}, u32[]{:S(2)}, u32[]{:S(2)}) collective-permute-start(f32[8,256]{1,0:T(8,128)S(1)} %moments.1), channel_id=1, source_target_pairs={{0,8},{1,9},{2,10},{3,11},{4,12},{5,13},{6,14},{7,15},{8,0},{9,1},... | collective-permute-start | bytes 24584 | tf_op jit(solution)/shard_map/ppermute | solution.py:34
  124.2 1.2 pad_maximum_fusion.1
  125.4 0.2 collective-permute-start.21
  125.6 1.2 collective-permute-start.20
  126.9 1.9 %collective-permute-start.27 = (f32[8,256]{1,0:T(8,128)S(1)}, f32[8,256]{1,0:T(8,128)S(1)}, u32[]{:S(2)}, u32[]{:S(2)}) collective-permute-start(f32[8,256]{1,0:T(8,128)S(1)} %pad_maximum_fusion.5), channel_id=1, source_target_pairs={{0,4},{1,5},{2,6},{3,7},{4,0},{5,1},{6,2},{7,3},{8,12},{9,13},{10,... | collective-permute-start | bytes 24584 | tf_op jit(solution)/shard_map/ppermute | solution.py:34
  128.8 1.6 %collective-permute-start.26 = (f32[8,256]{1,0:T(8,128)S(1)}, f32[8,256]{1,0:T(8,128)S(1)}, u32[]{:S(2)}, u32[]{:S(2)}) collective-permute-start(f32[8,256]{1,0:T(8,128)S(1)} %pad_maximum_fusion.5), channel_id=1, source_target_pairs={{0,6},{1,7},{2,0},{3,1},{4,2},{5,3},{6,4},{7,5},{8,14},{9,15},{10,... | collective-permute-start | bytes 24584 | tf_op jit(solution)/shard_map/ppermute | solution.py:34
  130.4 0.5 collective-permute-start.25
  130.9 0.1 collective-permute-done.27
  131.0 1.3 collective-permute-done.26
  132.3 2.1 %collective-permute-done.25 = f32[8,256]{1,0:T(8,128)S(1)} collective-permute-done((f32[8,256]{1,0:T(8,128)S(1)}, f32[8,256]{1,0:T(8,128)S(1)}, u32[]{:S(2)}, u32[]{:S(2)}) %collective-permute-start.25) | collective-permute-done | bytes 8224 | tf_op jit(solution)/shard_map/ppermute | solution.py:34
  134.4 0.6 pad_maximum_fusion.6
  135.0 2.8 %collective-permute-start.28 = (f32[8,256]{1,0:T(8,128)}, f32[8,256]{1,0:T(8,128)}, u32[]{:S(2)}, u32[]{:S(2)}) collective-permute-start(f32[8,256]{1,0:T(8,128)} %pad_maximum_fusion.6), channel_id=1, source_target_pairs={{0,1},{1,0},{2,3},{3,2},{4,5},{5,4},{6,7},{7,6},{8,9},{9,8},{10,11... | collective-permute-start | bytes 24584 | tf_op jit(solution)/shard_map/ppermute | solution.py:34
  137.8 0.1 stack.163.refs_1_
  137.9 1.5 collective-permute-done.21.refs_12_.refs_13_
  139.4 1.7 %collective-permute-start.23 = (bf16[96,960]{1,0:T(8,128)(2,1)S(1)}, bf16[96,960]{1,0:T(8,128)(2,1)S(1)}, u32[]{:S(2)}, u32[]{:S(2)}) collective-permute-start(bf16[96,960]{1,0:T(8,128)(2,1)S(1)} %slice.89), channel_id=1, source_target_pairs={{0,48},{16,0},{32,16},{48,32},{64,112},{80,64},{96,80},{112,96},{1... | collective-permute-start | bytes 552968 | tf_op jit(solution)/shard_map/ppermute | solution.py:38
  141.1 0.3 collective-permute-start.22
  141.5 0.8 add_multiply_fusion
  142.3 1.7 %collective-permute-done.23.refs_15_ = bf16[96,960]{1,0:T(8,128)(2,1)S(1)} collective-permute-done((bf16[96,960]{1,0:T(8,128)(2,1)S(1)}, bf16[96,960]{1,0:T(8,128)(2,1)S(1)}, u32[]{:S(2)}, u32[]{:S(2)}) %collective-permute-start.23) | collective-permute-done | bytes 184352 | tf_op jit(solution)/shard_map/ppermute | solution.py:38
  144.0 3.2 %collective-permute-done.22.refs_14_ = bf16[96,960]{1,0:T(8,128)(2,1)S(1)} collective-permute-done((bf16[96,960]{1,0:T(8,128)(2,1)S(1)}, bf16[96,960]{1,0:T(8,128)(2,1)S(1)}, u32[]{:S(2)}, u32[]{:S(2)}) %collective-permute-start.22) | collective-permute-done | bytes 184352 | tf_op jit(solution)/shard_map/ppermute | solution.py:38
  147.2 9.4 %project.1 = bf16[4,16,16,960]{3,2,1,0:T(8,128)(2,1)} custom-call(s32[16]{0:T(128)S(1)} %stack.154.refs_0_, s32[8]{0:T(128)S(1)} %stack.163.refs_1_, bf16[384,1536]{1,0:T(8,128)(2,1)S(1)} %pad_maximum_fusion.refs_1_.refs_2_, bf16[128,1536]{1,0:T(8,128)(2,1)} %constant_dynamic-update-slice_fusion.refs_2_.refs_3_, ...), custom_call_target="tpu_custom_call" | custom-call | flops 3000000000 | bytes 8000000 | tf_op jit(solution)/shard_map/project/pallas_call | solution.py:261
  (39 shorter events, 0.4 us)
Async XLA Ops:
  0.0 4.5 %copy-start.4 = (bf16[4,2,32,192]{3,2,1,0:T(8,128)(2,1)S(1)}, bf16[4,2,32,192]{3,2,1,0:T(8,128)(2,1)}, u32[]{:S(2)}) copy-start(bf16[4,2,32,192]{3,2,1,0:T(8,128)(2,1)} %own.1) | copy-start | bytes 294916
  0.0 23.6 %copy-start.3 = (bf16[192,384]{1,0:T(8,128)(2,1)S(1)}, bf16[192,384]{1,0:T(8,128)(2,1)}, u32[]{:S(2)}) copy-start(bf16[192,384]{1,0:T(8,128)(2,1)} %w_short.1) | copy-start | bytes 442372
  2.4 15.7 %collective-permute-start.12 = (bf16[192,320]{1,0:T(8,128)(2,1)}, bf16[192,320]{1,0:T(8,128)(2,1)S(1)}, u32[]{:S(2)}, u32[]{:S(2)}) collective-permute-start(bf16[192,320]{1,0:T(8,128)(2,1)} %get-tuple-element.10), channel_id=1, source_target_pairs={{0,8},{1,9},{2,10},{3,11},{4,12},{5,13},{6,14},{7,15},{8,0},{9,1},... | collective-permute-start | bytes 368648 | tf_op jit(solution)/shard_map/ppermute | solution.py:34
  4.5 16.5 %collective-permute-start.1 = (bf16[4,2,32,192]{3,2,1,0:T(8,128)(2,1)S(1)}, bf16[4,2,32,192]{3,2,1,0:T(8,128)(2,1)S(1)}, u32[]{:S(2)}, u32[]{:S(2)}) collective-permute-start(bf16[4,2,32,192]{3,2,1,0:T(8,128)(2,1)S(1)} %copy-done.4), channel_id=1, source_target_pairs={{0,15},{1,2},{2,1},{3,4},{4,3},{5,6},{6,5},{7,8},{8,7},{9,10},{10,... | collective-permute-start | bytes 294920 | tf_op jit(solution)/shard_map/ppermute | solution.py:34
  7.0 15.9 %collective-permute-start = (bf16[4,2,32,192]{3,2,1,0:T(8,128)(2,1)S(1)}, bf16[4,2,32,192]{3,2,1,0:T(8,128)(2,1)S(1)}, u32[]{:S(2)}, u32[]{:S(2)}) collective-permute-start(bf16[4,2,32,192]{3,2,1,0:T(8,128)(2,1)S(1)} %copy-done.4), channel_id=1, source_target_pairs={{0,1},{1,0},{2,3},{3,2},{4,5},{5,4},{6,7},{7,6},{8,9},{9,8},{10,11... | collective-permute-start | bytes 294920 | tf_op jit(solution)/shard_map/ppermute | solution.py:34
  8.6 8.8 %collective-permute-start.2 = (bf16[4,2,32,192]{3,2,1,0:T(8,128)(2,1)S(1)}, bf16[4,2,32,192]{3,2,1,0:T(8,128)(2,1)S(1)}, u32[]{:S(2)}, u32[]{:S(2)}) collective-permute-start(bf16[4,2,32,192]{3,2,1,0:T(8,128)(2,1)S(1)} %copy-done.4), channel_id=1, source_target_pairs={{0,16},{16,32},{32,48},{48,64},{64,80},{80,96},{96,112},{112,0},{1... | collective-permute-start | bytes 294920 | tf_op jit(solution)/shard_map/ppermute | solution.py:38
  17.4 6.2 %collective-permute-start.4 = (bf16[4,2,32,192]{3,2,1,0:T(8,128)(2,1)S(1)}, bf16[4,2,32,192]{3,2,1,0:T(8,128)(2,1)S(1)}, u32[]{:S(2)}, u32[]{:S(2)}) collective-permute-start(bf16[4,2,32,192]{3,2,1,0:T(8,128)(2,1)S(1)} %collective-permute-done.2.back), channel_id=1, source_target_pairs={{0,15},{1,2},{2,1},{3,4},{4,3},{5,6},{6,5},{7,8},{8,7},{9,10},{10,... | collective-permute-start | bytes 294920 | tf_op jit(solution)/shard_map/ppermute | solution.py:34
  18.1 5.5 %collective-permute-start.3 = (bf16[4,2,32,192]{3,2,1,0:T(8,128)(2,1)S(1)}, bf16[4,2,32,192]{3,2,1,0:T(8,128)(2,1)S(1)}, u32[]{:S(2)}, u32[]{:S(2)}) collective-permute-start(bf16[4,2,32,192]{3,2,1,0:T(8,128)(2,1)S(1)} %collective-permute-done.2.back), channel_id=1, source_target_pairs={{0,1},{1,0},{2,3},{3,2},{4,5},{5,4},{6,7},{7,6},{8,9},{9,8},{10,11... | collective-permute-start | bytes 294920 | tf_op jit(solution)/shard_map/ppermute | solution.py:34
  19.1 34.6 %collective-permute-start.15 = (bf16[2,192,320]{2,1,0:T(8,128)(2,1)S(1)}, bf16[2,192,320]{2,1,0:T(8,128)(2,1)S(1)}, u32[]{:S(2)}, u32[]{:S(2)}) collective-permute-start(bf16[2,192,320]{2,1,0:T(8,128)(2,1)S(1)} %pad_maximum_fusion.4), channel_id=1, source_target_pairs={{0,4},{1,5},{2,6},{3,7},{4,0},{5,1},{6,2},{7,3},{8,12},{9,13},{10,... | collective-permute-start | bytes 737288 | tf_op jit(solution)/shard_map/ppermute | solution.py:34
  21.0 32.6 %collective-permute-start.14 = (bf16[2,192,320]{2,1,0:T(8,128)(2,1)S(1)}, bf16[2,192,320]{2,1,0:T(8,128)(2,1)S(1)}, u32[]{:S(2)}, u32[]{:S(2)}) collective-permute-start(bf16[2,192,320]{2,1,0:T(8,128)(2,1)S(1)} %pad_maximum_fusion.4), channel_id=1, source_target_pairs={{0,6},{1,7},{2,0},{3,1},{4,2},{5,3},{6,4},{7,5},{8,14},{9,15},{10,... | collective-permute-start | bytes 737288 | tf_op jit(solution)/shard_map/ppermute | solution.py:34
  22.9 24.0 %collective-permute-start.13 = (bf16[2,192,320]{2,1,0:T(8,128)(2,1)S(1)}, bf16[2,192,320]{2,1,0:T(8,128)(2,1)S(1)}, u32[]{:S(2)}, u32[]{:S(2)}) collective-permute-start(bf16[2,192,320]{2,1,0:T(8,128)(2,1)S(1)} %pad_maximum_fusion.4), channel_id=1, source_target_pairs={{0,2},{1,3},{2,4},{3,5},{4,6},{5,7},{6,0},{7,1},{8,10},{9,11},{10,... | collective-permute-start | bytes 737288 | tf_op jit(solution)/shard_map/ppermute | solution.py:34
  23.6 3.3 %copy-start.1 = (bf16[3,3,3,384,384]{4,3,2,1,0:T(8,128)(2,1)S(1)}, bf16[3,3,3,384,384]{4,3,2,1,0:T(8,128)(2,1)}, u32[]{:S(2)}) copy-start(bf16[3,3,3,384,384]{4,3,2,1,0:T(8,128)(2,1)} %param.8) | copy-start | bytes 23887876
  26.9 2.1 %copy-start.2 = (bf16[3,3,3,192,384]{4,3,2,1,0:T(8,128)(2,1)S(1)}, bf16[3,3,3,192,384]{4,3,2,1,0:T(8,128)(2,1)}, u32[]{:S(2)}) copy-start(bf16[3,3,3,192,384]{4,3,2,1,0:T(8,128)(2,1)} %param.7) | copy-start | bytes 11943940
  46.4 4.6 %collective-permute-start.5 = (bf16[64,1536]{1,0:T(8,128)(2,1)S(1)}, bf16[64,1536]{1,0:T(8,128)(2,1)S(1)}, u32[]{:S(2)}, u32[]{:S(2)}) collective-permute-start(bf16[64,1536]{1,0:T(8,128)(2,1)S(1)} %convolutions.1), channel_id=1, source_target_pairs={{0,8},{1,9},{2,10},{3,11},{4,12},{5,13},{6,14},{7,15},{8,0},{9,1},... | collective-permute-start | bytes 589832 | tf_op jit(solution)/shard_map/ppermute | solution.py:34
  51.1 12.5 %collective-permute-start.7 = (bf16[128,1536]{1,0:T(8,128)(2,1)S(1)}, bf16[128,1536]{1,0:T(8,128)(2,1)S(1)}, u32[]{:S(2)}, u32[]{:S(2)}) collective-permute-start(bf16[128,1536]{1,0:T(8,128)(2,1)S(1)} %pad_maximum_fusion.3), channel_id=1, source_target_pairs={{0,6},{1,7},{2,0},{3,1},{4,2},{5,3},{6,4},{7,5},{8,14},{9,15},{10,... | collective-permute-start | bytes 1179656 | tf_op jit(solution)/shard_map/ppermute | solution.py:34
  53.6 9.3 %collective-permute-start.6 = (bf16[128,1536]{1,0:T(8,128)(2,1)S(1)}, bf16[128,1536]{1,0:T(8,128)(2,1)S(1)}, u32[]{:S(2)}, u32[]{:S(2)}) collective-permute-start(bf16[128,1536]{1,0:T(8,128)(2,1)S(1)} %pad_maximum_fusion.3), channel_id=1, source_target_pairs={{0,2},{1,3},{2,4},{3,5},{4,6},{5,7},{6,0},{7,1},{8,10},{9,11},{10,... | collective-permute-start | bytes 1179656 | tf_op jit(solution)/shard_map/ppermute | solution.py:34
  53.8 38.2 %collective-permute-start.16 = (bf16[8,192,320]{2,1,0:T(8,128)(2,1)S(1)}, bf16[8,192,320]{2,1,0:T(8,128)(2,1)}, u32[]{:S(2)}, u32[]{:S(2)}) collective-permute-start(bf16[8,192,320]{2,1,0:T(8,128)(2,1)S(1)} %constant_dynamic-update-slice_fusion.2.same), channel_id=1, source_target_pairs={{0,1},{1,0},{2,3},{3,2},{4,5},{5,4},{6,7},{7,6},{8,9},{9,8},{10,11... | collective-permute-start | bytes 2949128 | tf_op jit(solution)/shard_map/ppermute | solution.py:34
  63.6 22.6 %collective-permute-start.8 = (bf16[64,1536]{1,0:T(8,128)(2,1)}, bf16[64,1536]{1,0:T(8,128)(2,1)}, u32[]{:S(2)}, u32[]{:S(2)}) collective-permute-start(bf16[64,1536]{1,0:T(8,128)(2,1)} %slice.84), channel_id=1, source_target_pairs={{0,2},{1,3},{2,4},{3,5},{4,6},{5,7},{6,0},{7,1},{8,10},{9,11},{10,... | collective-permute-start | bytes 589832 | tf_op jit(solution)/shard_map/ppermute | solution.py:34
  63.6 0.7 copy-start.5
  64.3 52.5 %collective-permute-start.10 = (bf16[384,1536]{1,0:T(8,128)(2,1)S(1)}, bf16[384,1536]{1,0:T(8,128)(2,1)}, u32[]{:S(2)}, u32[]{:S(2)}) collective-permute-start(bf16[384,1536]{1,0:T(8,128)(2,1)S(1)} %pad_maximum_fusion.refs_1_.refs_2_), channel_id=1, source_target_pairs={{0,1},{1,0},{2,3},{3,2},{4,5},{5,4},{6,7},{7,6},{8,9},{9,8},{10,11... | collective-permute-start | bytes 3538952 | tf_op jit(solution)/shard_map/ppermute | solution.py:34
  83.1 7.4 %collective-permute-start.9 = (bf16[64,1536]{1,0:T(8,128)(2,1)S(1)}, bf16[64,1536]{1,0:T(8,128)(2,1)S(1)}, u32[]{:S(2)}, u32[]{:S(2)}) collective-permute-start(bf16[64,1536]{1,0:T(8,128)(2,1)S(1)} %slice.85), channel_id=1, source_target_pairs={{0,6},{1,7},{2,0},{3,1},{4,2},{5,3},{6,4},{7,5},{8,14},{9,15},{10,... | collective-permute-start | bytes 589832 | tf_op jit(solution)/shard_map/ppermute | solution.py:34
  91.2 25.6 %collective-permute-start.11 = (bf16[128,1536]{1,0:T(8,128)(2,1)}, bf16[128,1536]{1,0:T(8,128)(2,1)}, u32[]{:S(2)}, u32[]{:S(2)}) collective-permute-start(bf16[128,1536]{1,0:T(8,128)(2,1)} %constant_dynamic-update-slice_fusion.refs_2_.refs_3_), channel_id=1, source_target_pairs={{0,1},{1,0},{2,3},{3,2},{4,5},{5,4},{6,7},{7,6},{8,9},{9,8},{10,11... | collective-permute-start | bytes 1179656 | tf_op jit(solution)/shard_map/ppermute | solution.py:34
  91.9 4.0 %copy-start = (bf16[5120,960]{1,0:T(8,128)(2,1)S(1)}, bf16[5120,960]{1,0:T(8,128)(2,1)}, u32[]{:S(2)}) copy-start(bf16[5120,960]{1,0:T(8,128)(2,1)} %copy.8.w_qkv) | copy-start | bytes 29491204
  104.6 11.0 %collective-permute-start.18 = (bf16[192,960]{1,0:T(8,128)(2,1)}, bf16[192,960]{1,0:T(8,128)(2,1)S(1)}, u32[]{:S(2)}, u32[]{:S(2)}) collective-permute-start(bf16[192,960]{1,0:T(8,128)(2,1)} %fold.1.refs_6_), channel_id=1, source_target_pairs={{0,48},{16,0},{32,16},{48,32},{64,112},{80,64},{96,80},{112,96},{1... | collective-permute-start | bytes 1105928 | tf_op jit(solution)/shard_map/ppermute | solution.py:38
  104.6 12.2 %collective-permute-start.17 = (bf16[192,960]{1,0:T(8,128)(2,1)}, bf16[192,960]{1,0:T(8,128)(2,1)S(1)}, u32[]{:S(2)}, u32[]{:S(2)}) collective-permute-start(bf16[192,960]{1,0:T(8,128)(2,1)} %fold.1.refs_6_), channel_id=1, source_target_pairs={{0,16},{16,32},{32,48},{48,0},{64,80},{80,96},{96,112},{112,64},{1... | collective-permute-start | bytes 1105928 | tf_op jit(solution)/shard_map/ppermute | solution.py:38
  106.0 18.2 %collective-permute-start.19 = (bf16[192,960]{1,0:T(8,128)(2,1)}, bf16[192,960]{1,0:T(8,128)(2,1)S(1)}, u32[]{:S(2)}, u32[]{:S(2)}) collective-permute-start(bf16[192,960]{1,0:T(8,128)(2,1)} %fold.1.refs_6_), channel_id=1, source_target_pairs={{0,64},{16,80},{32,96},{48,112},{64,0},{80,16},{96,32},{112,48},{1... | collective-permute-start | bytes 1105928 | tf_op jit(solution)/shard_map/ppermute | solution.py:38
  122.6 4.3 %collective-permute-start.24 = (f32[8,256]{1,0:T(8,128)S(1)}, f32[8,256]{1,0:T(8,128)S(1)}, u32[]{:S(2)}, u32[]{:S(2)}) collective-permute-start(f32[8,256]{1,0:T(8,128)S(1)} %moments.1), channel_id=1, source_target_pairs={{0,8},{1,9},{2,10},{3,11},{4,12},{5,13},{6,14},{7,15},{8,0},{9,1},... | collective-permute-start | bytes 24584 | tf_op jit(solution)/shard_map/ppermute | solution.py:34
  125.4 14.0 %collective-permute-start.21 = (bf16[288,960]{1,0:T(8,128)(2,1)}, bf16[288,960]{1,0:T(8,128)(2,1)S(1)}, u32[]{:S(2)}, u32[]{:S(2)}) collective-permute-start(bf16[288,960]{1,0:T(8,128)(2,1)} %get-tuple-element.11), channel_id=1, source_target_pairs={{0,48},{16,0},{32,16},{48,32},{64,112},{80,64},{96,80},{112,96},{1... | collective-permute-start | bytes 1658888 | tf_op jit(solution)/shard_map/ppermute | solution.py:38
  125.6 15.5 %collective-permute-start.20 = (bf16[288,960]{1,0:T(8,128)(2,1)}, bf16[288,960]{1,0:T(8,128)(2,1)S(1)}, u32[]{:S(2)}, u32[]{:S(2)}) collective-permute-start(bf16[288,960]{1,0:T(8,128)(2,1)} %get-tuple-element.12), channel_id=1, source_target_pairs={{0,16},{16,32},{32,48},{48,0},{64,80},{80,96},{96,112},{112,64},{1... | collective-permute-start | bytes 1658888 | tf_op jit(solution)/shard_map/ppermute | solution.py:38
  126.9 4.1 %collective-permute-start.27 = (f32[8,256]{1,0:T(8,128)S(1)}, f32[8,256]{1,0:T(8,128)S(1)}, u32[]{:S(2)}, u32[]{:S(2)}) collective-permute-start(f32[8,256]{1,0:T(8,128)S(1)} %pad_maximum_fusion.5), channel_id=1, source_target_pairs={{0,4},{1,5},{2,6},{3,7},{4,0},{5,1},{6,2},{7,3},{8,12},{9,13},{10,... | collective-permute-start | bytes 24584 | tf_op jit(solution)/shard_map/ppermute | solution.py:34
  128.8 3.5 %collective-permute-start.26 = (f32[8,256]{1,0:T(8,128)S(1)}, f32[8,256]{1,0:T(8,128)S(1)}, u32[]{:S(2)}, u32[]{:S(2)}) collective-permute-start(f32[8,256]{1,0:T(8,128)S(1)} %pad_maximum_fusion.5), channel_id=1, source_target_pairs={{0,6},{1,7},{2,0},{3,1},{4,2},{5,3},{6,4},{7,5},{8,14},{9,15},{10,... | collective-permute-start | bytes 24584 | tf_op jit(solution)/shard_map/ppermute | solution.py:34
  130.4 4.0 %collective-permute-start.25 = (f32[8,256]{1,0:T(8,128)S(1)}, f32[8,256]{1,0:T(8,128)S(1)}, u32[]{:S(2)}, u32[]{:S(2)}) collective-permute-start(f32[8,256]{1,0:T(8,128)S(1)} %pad_maximum_fusion.5), channel_id=1, source_target_pairs={{0,2},{1,3},{2,4},{3,5},{4,6},{5,7},{6,0},{7,1},{8,10},{9,11},{10,... | collective-permute-start | bytes 24584 | tf_op jit(solution)/shard_map/ppermute | solution.py:34
  135.0 6.4 %collective-permute-start.28 = (f32[8,256]{1,0:T(8,128)}, f32[8,256]{1,0:T(8,128)}, u32[]{:S(2)}, u32[]{:S(2)}) collective-permute-start(f32[8,256]{1,0:T(8,128)} %pad_maximum_fusion.6), channel_id=1, source_target_pairs={{0,1},{1,0},{2,3},{3,2},{4,5},{5,4},{6,7},{7,6},{8,9},{9,8},{10,11... | collective-permute-start | bytes 24584 | tf_op jit(solution)/shard_map/ppermute | solution.py:34
  139.4 4.6 %collective-permute-start.23 = (bf16[96,960]{1,0:T(8,128)(2,1)S(1)}, bf16[96,960]{1,0:T(8,128)(2,1)S(1)}, u32[]{:S(2)}, u32[]{:S(2)}) collective-permute-start(bf16[96,960]{1,0:T(8,128)(2,1)S(1)} %slice.89), channel_id=1, source_target_pairs={{0,48},{16,0},{32,16},{48,32},{64,112},{80,64},{96,80},{112,96},{1... | collective-permute-start | bytes 552968 | tf_op jit(solution)/shard_map/ppermute | solution.py:38
  141.1 6.1 %collective-permute-start.22 = (bf16[96,960]{1,0:T(8,128)(2,1)S(1)}, bf16[96,960]{1,0:T(8,128)(2,1)S(1)}, u32[]{:S(2)}, u32[]{:S(2)}) collective-permute-start(bf16[96,960]{1,0:T(8,128)(2,1)S(1)} %slice.88), channel_id=1, source_target_pairs={{0,16},{16,32},{32,48},{48,0},{64,80},{80,96},{96,112},{112,64},{1... | collective-permute-start | bytes 552968 | tf_op jit(solution)/shard_map/ppermute | solution.py:38

commit v2 on v0

v2 whole, which is shorter than its diff:
```python
import jax
import jax.numpy as jnp
from jax import lax
from jax.experimental import pallas as pl
from jax.experimental.pallas import tpu as pltpu
from jax.sharding import PartitionSpec as P

F32 = jnp.float32
BF16 = jnp.bfloat16
MIB = 1 << 20

FRAMES_PAIRS = 8
ROWS_PAIRS = 16


def along_x(by):
    return [(i, i // 4 * 4 + (i + by) % 4) for i in range(FRAMES_PAIRS)]


SWAP_Y_HI = [(i, i ^ 4) for i in range(FRAMES_PAIRS)]
NEXT_FRAMES = [(i, (i + 1) % FRAMES_PAIRS) for i in range(FRAMES_PAIRS)]


def along_z(by):
    return [(i, i // 8 * 8 + (i + 2 * by) % 8) for i in range(ROWS_PAIRS)]


SWAP_Z, SWAP_Z_RING = ([(i, i ^ 2) for i in range(ROWS_PAIRS)], [(i, i ^ 6) for i in range(ROWS_PAIRS)])


SWAP_Y_LO = [(i, i ^ 8) for i in range(ROWS_PAIRS)]
SWAP_CORE = [(i, i ^ 1) for i in range(ROWS_PAIRS)]
SWAP_CHIP = [(i, (i + 1) % ROWS_PAIRS if i % 2 else (i - 1) % ROWS_PAIRS) for i in range(ROWS_PAIRS)]
NEXT_FRAMES_SWAP_CHIP = [(a * ROWS_PAIRS + c, b * ROWS_PAIRS + d) for a, b in NEXT_FRAMES for c, d in SWAP_CHIP]


def by_rows(x, pairs):
    return lax.ppermute(x, "rows", pairs)


def by_frames(x, pairs):
    return lax.ppermute(x, "frames", pairs)


def here():
    return lax.axis_index("frames"), lax.axis_index("rows")


def at_chip(place, y_lo, z):
    rows = place[1]
    return (rows // 8 + y_lo) % 2 * 4 + (rows // 2 + z) % 4


def at_rows(place, y_lo, z, core):
    return at_chip(place, y_lo, z) * 2 + (place[1] + core) % 2


def at_frames(place, y_hi, x):
    return (place[0] // 4 + y_hi) % 2 * 4 + (place[0] + x) % 4


def whole(memory=pltpu.VMEM):
    return pl.BlockSpec(memory_space=memory)


def in_hbm(*arrays):
    return [pltpu.with_memory_space_constraint(array, pltpu.HBM) for array in arrays]


def in_vmem(*arrays):
    return [pltpu.with_memory_space_constraint(array, pltpu.VMEM) for array in arrays]


def normalized_silu(v):
    u = v * lax.rsqrt(jnp.mean(v * v, axis=-1, keepdims=True) + 1e-06)
    half = 0.5 * u
    return half + half * jnp.tanh(half)


def over_columns(v):
    n, c = v.shape[0], v.shape[1] // 3
    col = lax.broadcasted_iota(jnp.int32, (n, c), 0) & 31
    before = jnp.where(col == 0, 0.0, pltpu.roll(v[:, :c], 1, 0))
    after = jnp.where(col == 31, 0.0, pltpu.roll(v[:, 2 * c :], n - 1, 0))
    return v[:, c : 2 * c] + before + after


def taps(ref, frames, rows):
    n, c = frames * rows * 32, ref.shape[-1]
    windows = [ref[t : t + frames, i : i + rows].reshape(n, c) for t in range(3) for i in range(3)]
    return jnp.concatenate(windows, axis=1)


def conv_kernel(
    side_core, side_chip, back, back_core, back_chip, video, w_in, w_out, shortcut,
    out, first, second, vin, vout, flat, own, w_short, sems,
):
    place = here()
    core = place[1] % 2
    at_first_frames, at_first_rows, at_last_rows = (place[0] == 0, place[1] == 0, place[1] == 15)
    small = [pltpu.make_async_copy(video, own, sems.at[54]), pltpu.make_async_copy(shortcut, w_short, sems.at[55])]
    for load in small:
        load.start()
    loads = []
    for n, (source, target, size) in enumerate(((w_in, vin, 192), (w_out, vout, 384))):
        loads.append(
            [
                pltpu.make_async_copy(
                    source.at[3 * k + j],
                    target.at[pl.ds(size * k, size), pl.ds(384 * j, 384)],
                    sems.at[27 * n + 3 * k + j],
                )
                for k in range(9)
                for j in range(3)
            ]
        )
    for load in loads[0]:
        load.start()

    core_row = jnp.where(core == 0, 4, 0)
    chip_row = 4 - core_row
    for frame, blocks in ((0, (back, back_core, back_chip)), (4, (own, side_core, side_chip))):
        for ref, row in zip(blocks, (2, core_row, chip_row)):
            if ref is own:
                small[0].wait()
            v = normalized_silu(ref[...].astype(F32).reshape(256, 192))
            first[pl.ds(frame, 4), pl.ds(row, 2)] = v.astype(BF16).reshape(4, 2, 32, 192)

    @pl.when(at_first_frames)
    def _():
        first[0:4] = jnp.zeros((4, 6, 32, 192), BF16)

    @pl.when(at_first_rows)
    def _():
        first[:, 0:2] = jnp.zeros((8, 2, 32, 192), BF16)

    @pl.when(at_last_rows)
    def _():
        first[:, 4:6] = jnp.zeros((8, 2, 32, 192), BF16)

    for load in loads[0]:
        load.wait()
    for load in loads[1]:
        load.start()
    acc = over_columns(jnp.dot(taps(first, 6, 4), vin[...], preferred_element_type=F32))
    second[...] = normalized_silu(acc).astype(BF16).reshape(6, 4, 32, 384)

    @pl.when(at_first_frames)
    def _():
        second[0:2] = jnp.zeros((2, 4, 32, 384), BF16)

    @pl.when(at_first_rows)
    def _():
        second[:, 0:1] = jnp.zeros((6, 1, 32, 384), BF16)

    @pl.when(at_last_rows)
    def _():
        second[:, 3:4] = jnp.zeros((6, 1, 32, 384), BF16)

    for load in loads[1]:
        load.wait()
    acc = over_columns(jnp.dot(taps(second, 4, 2), vout[...], preferred_element_type=F32))
    small[1].wait()
    acc = acc + jnp.dot(own[...].reshape(256, 192), w_short[...], preferred_element_type=F32)
    for n in range(3):
        flat[n] = acc[:, 128 * n : 128 * (n + 1)].reshape(8, 32, 128)
    for f in range(4):
        for a in range(2):
            for b in range(2):
                for n in range(3):
                    part = 384 * (2 * a + b) + 128 * n
                    cols = flat[n, 2 * f + a, pl.ds(b, 16, stride=2), :]
                    out[16 * f : 16 * (f + 1), part : part + 128] = cols.astype(BF16)


def convolutions(video, blocks, w_in, w_out, w_short):
    return pl.pallas_call(
        conv_kernel,
        out_shape=pltpu.VMEM((64, 1536), BF16),
        in_specs=[whole()] * 5 + [whole(pltpu.HBM)] * 4,
        out_specs=whole(),
        scratch_shapes=[
            pltpu.VMEM((8, 6, 32, 192), BF16),
            pltpu.VMEM((6, 4, 32, 384), BF16),
            pltpu.VMEM((1728, 1152), BF16),
            pltpu.VMEM((3456, 1152), BF16),
            pltpu.VMEM((3, 8, 32, 128), F32),
            pltpu.VMEM((4, 2, 32, 192), BF16),
            pltpu.VMEM((192, 384), BF16),
            pltpu.SemaphoreType.DMA((56,)),
        ],
        compiler_params=pltpu.CompilerParams(vmem_limit_bytes=40 * MIB),
        cost_estimate=pl.CostEstimate(flops=8 * 10**9, bytes_accessed=13 * 10**6, transcendentals=10**6),
        name="convolutions",
    )(*in_vmem(*blocks), *in_hbm(video, w_in.reshape(27, 192, 384), w_out.reshape(27, 384, 384), w_short))


def fold_kernel(*refs):
    place = here()
    count = (len(refs) - 3) // 2
    w_qkv, out, rows = refs[2 * count :]
    core = place[1] % 2
    rows[:, 128:] = jnp.ones((5120, 128), BF16)
    chips = []
    for same, other in zip(refs[:count], refs[count : 2 * count]):
        for n in range(same.shape[0] // 480):
            s = len(chips)
            chips.append(at_chip(place, s // 4, (0, -1, 1, 2)[s % 4]))
            for ref, at in ((same, core), (other, 1 - core)):
                block = ref[480 * n : 480 * (n + 1)]
                first = pl.multiple_of(640 * s + 320 * at, 32)
                rows[pl.ds(first, 320), :128] = block[:320]
                rows[pl.ds(first, 160), 128:192] = block[320:, :64]
                rows[pl.ds(first + 160, 160), 128:192] = block[320:, 64:]
    total, mean = None, None
    for s, chip in enumerate(chips):
        slab, part = w_qkv[:, pl.ds(pl.multiple_of(chip * 640, 128), 640)], rows[640 * s : 640 * (s + 1)]
        term = jnp.dot(slab, part, preferred_element_type=F32)
        part = jnp.sum(part.astype(F32), axis=0, keepdims=True)
        total = term if total is None else total + term
        mean = part if mean is None else mean + part
    total = total - total[:, 192:193] * (mean * (1.0 / 5120))
    turned = jnp.concatenate([total, jnp.zeros((64, 256), F32)], axis=0).T
    out[...] = turned[:192, :960].astype(BF16)


def fold(same, other, w_qkv):
    return pl.pallas_call(
        fold_kernel,
        out_shape=pltpu.VMEM((192, 960), BF16),
        in_specs=[whole()] * (2 * len(same) + 1),
        out_specs=whole(),
        scratch_shapes=[pltpu.VMEM((5120, 256), BF16)],
        compiler_params=pltpu.CompilerParams(vmem_limit_bytes=20 * MIB),
        cost_estimate=pl.CostEstimate(flops=4 * 10**9, bytes_accessed=12 * 10**6, transcendentals=0),
        name="fold",
    )(*in_vmem(*same, *other, w_qkv.T))


def moments_kernel(layout, *refs):
    place = here()
    count = len(layout)
    pieces, w_embed, out, tokens = (refs[:count], refs[count], refs[count + 1], refs[count + 2])
    for ref, parts in zip(pieces, layout):
        for source, size, block, at in parts:
            tokens[at_rows(place, *block), at : at + size] = ref[source : source + size]
    for g in range(4):
        e = lax.dot_general(
            w_embed[...],
            tokens[4 * g : 4 * g + 4].reshape(256, 1536),
            (((1,), (1,)), ((), ())),
            preferred_element_type=F32,
        )
        mean = jnp.mean(e, axis=0, keepdims=True)
        out[g : g + 1, :] = mean
        out[4 + g : 5 + g, :] = jnp.sum((e - mean) * (e - mean), axis=0, keepdims=True)


def moments(pieces, layout, w_embed):
    return pl.pallas_call(
        lambda *refs: moments_kernel(layout, *refs),
        out_shape=[pltpu.VMEM((8, 256), F32), pltpu.VMEM((16, 64, 1536), BF16)],
        in_specs=[whole()] * (len(pieces) + 1),
        out_specs=[whole(), whole()],
        compiler_params=pltpu.CompilerParams(vmem_limit_bytes=20 * MIB),
        cost_estimate=pl.CostEstimate(flops=2 * 10**9, bytes_accessed=5 * 10**6, transcendentals=0),
        name="moments",
    )(*in_vmem(*pieces), w_embed.T)


def merge_kernel(features, *refs):
    parts, out = [ref[...] for ref in refs[:-1]], refs[-1]
    mean = sum(part[:4] for part in parts) * (1.0 / len(parts))
    spread = sum(part[4:] for part in parts)
    spread = spread + features * sum((part[:4] - mean) * (part[:4] - mean) for part in parts)
    out[:4] = mean
    out[4:] = spread


def merged(parts, features):
    return pl.pallas_call(
        lambda *refs: merge_kernel(features, *refs),
        out_shape=pltpu.VMEM((8, 256), F32),
        in_specs=[whole()] * len(parts),
        out_specs=whole(),
        compiler_params=pltpu.CompilerParams(vmem_limit_bytes=2 * MIB),
        cost_estimate=pl.CostEstimate(flops=10**6, bytes_accessed=10**5, transcendentals=0),
        name="merge",
    )(*in_vmem(*parts))


def most_kernel(layout, tokens, *refs):
    place = here()
    count = len(layout)
    weights, out, folded = (refs[:count], refs[count], refs[count + 1])
    for ref, parts in zip(weights, layout):
        for source, size, block, at in parts:
            folded[pl.ds(pl.multiple_of(at_frames(place, *block) * 192 + at, 96), size), :] = ref[source : source + size]
    folded[pl.ds(pl.multiple_of(at_frames(place, 1, 2) * 192, 192), 192), :] = jnp.zeros((192, 960), BF16)
    for g in range(4):
        x = tokens[4 * g : 4 * g + 4].reshape(256, 1536)
        out[256 * g : 256 * (g + 1)] = jnp.dot(x, folded[...], preferred_element_type=F32)


def project_most(tokens, weights, layout):
    return pl.pallas_call(
        lambda *refs: most_kernel(layout, *refs),
        out_shape=pltpu.VMEM((1024, 960), F32),
        in_specs=[whole()] * (len(weights) + 1),
        out_specs=whole(),
        scratch_shapes=[pltpu.VMEM((1536, 960), BF16)],
        compiler_params=pltpu.CompilerParams(vmem_limit_bytes=20 * MIB),
        cost_estimate=pl.CostEstimate(flops=4 * 10**9, bytes_accessed=8 * 10**6, transcendentals=0),
        name="project_most",
    )(*in_vmem(tokens, *weights))


def last_kernel(tokens, total, low, high, stats, out, folded, staged, sems):
    place = here()
    last = at_frames(place, 1, 2)
    pair, half = last // 2, last % 2
    folded[...] = jnp.zeros((384, 960), BF16)
    folded[pl.ds(pl.multiple_of(half * 192, 192), 96), :] = low[...]
    folded[pl.ds(pl.multiple_of(half * 192 + 96, 96), 96), :] = high[...]
    copies = []
    for g in range(4):
        x = tokens[4 * g : 4 * g + 4, :, pl.ds(pl.multiple_of(pair * 384, 128), 384)].reshape(256, 384)
        acc = total[256 * g : 256 * (g + 1)] + jnp.dot(x, folded[...], preferred_element_type=F32)
        scale = lax.rsqrt(stats[4 + g : 5 + g, :] * (1.0 / 5120) + 1e-06)
        scale = jnp.broadcast_to(scale, (128, 256)).T[:, :1]
        result = (acc * scale).astype(BF16).reshape(4, 4, 16, 960)
        for r in range(4):
            staged[:, 4 * g + r] = result[r]
        copies.append(
            pltpu.make_async_copy(staged.at[:, pl.ds(4 * g, 4)], out.at[:, pl.ds(4 * g, 4)], sems.at[g])
        )
        copies[g].start()
    for copy in copies:
        copy.wait()


def project_last(tokens, total, low, high, stats):
    return pl.pallas_call(
        last_kernel,
        out_shape=jax.ShapeDtypeStruct((4, 16, 16, 960), BF16),
        in_specs=[whole()] * 5,
        out_specs=whole(pltpu.HBM),
        scratch_shapes=[
            pltpu.VMEM((384, 960), BF16),
            pltpu.VMEM((4, 16, 16, 960), BF16),
            pltpu.SemaphoreType.DMA((4,)),
        ],
        compiler_params=pltpu.CompilerParams(vmem_limit_bytes=32 * MIB),
        cost_estimate=pl.CostEstimate(flops=2 * 10**9, bytes_accessed=8 * 10**6, transcendentals=0),
        name="project_last",
    )(*in_vmem(tokens, total, low, high, stats))


def slice_kernel(w_embed, out, slab, sem):
    place = here()
    load = pltpu.make_async_copy(w_embed.at[:, pl.ds(pl.multiple_of(place[0] // 2 * 384, 128), 384)], slab, sem)
    load.start()
    load.wait()
    mine = jnp.where(place[0] % 2 == 0, slab[:, :192], slab[:, 192:])
    out[:320] = mine[:, :128]
    out[320:] = jnp.concatenate([mine[:160, 128:], mine[160:, 128:]], axis=1)


def spliced(name, *targets):
    arrays = []
    for array in [part[0] for target in targets for part in target]:
        if not any(array is other for other in arrays):
            arrays.append(array)
    places = [[next(n for n, a in enumerate(arrays) if a is part[0]) for part in target] for target in targets]

    def kernel(*refs):
        for out, target, sources in zip(refs[len(arrays) :], targets, places):
            at = 0
            for (_, start, size), n in zip(target, sources):
                out[at : at + size] = refs[n][start : start + size]
                at += size

    rows = [sum(part[2] for part in target) for target in targets]
    columns = targets[0][0][0].shape[1]
    return pl.pallas_call(
        kernel,
        out_shape=[pltpu.VMEM((n, columns), BF16) for n in rows],
        in_specs=[whole()] * len(arrays),
        out_specs=[whole()] * len(targets),
        compiler_params=pltpu.CompilerParams(vmem_limit_bytes=8 * MIB),
        cost_estimate=pl.CostEstimate(flops=10**6, bytes_accessed=10**6, transcendentals=0),
        name=name,
    )(*in_vmem(*arrays))


def embed_slice(w_embed):
    return pl.pallas_call(
        slice_kernel,
        out_shape=pltpu.VMEM((480, 128), BF16),
        in_specs=[whole(pltpu.HBM)],
        out_specs=whole(),
        scratch_shapes=[pltpu.VMEM((320, 384), BF16), pltpu.SemaphoreType.DMA],
        cost_estimate=pl.CostEstimate(flops=10**6, bytes_accessed=10**6, transcendentals=0),
        name="embed_slice",
    )(*in_hbm(w_embed.T))


def shards(video, w_conv_in, w_conv_out, w_shortcut, w_embed, w_qkv):
    back = by_frames(video, NEXT_FRAMES)
    back_chip = lax.ppermute(video, ("frames", "rows"), NEXT_FRAMES_SWAP_CHIP)
    side_core, side_chip = by_rows(video, SWAP_CORE), by_rows(video, SWAP_CHIP)
    mine = embed_slice(w_embed)
    along = [by_rows(mine, along_z(by)) for by in (1, -1, 2)]
    along, back, back_chip, side_chip = lax.optimization_barrier((along, back, back_chip, side_chip))
    back_core = by_rows(back, SWAP_CORE)
    (four,) = spliced("embed_four", [(mine, 0, 480)] + [(part, 0, 480) for part in along])
    patches = convolutions(
        video, (side_core, side_chip, back, back_core, back_chip), w_conv_in, w_conv_out, w_shortcut
    )
    across = by_rows(four, SWAP_Y_LO)
    across, patches = lax.optimization_barrier((across, patches))
    folded = fold([four, across], [by_rows(four, SWAP_CORE), by_rows(across, SWAP_CORE)], w_qkv)

    opposite = by_rows(patches, SWAP_Y_LO)
    opposite, folded = lax.optimization_barrier((opposite, folded))
    (pair,) = spliced("patch_pair", [(patches, 0, 64), (opposite, 0, 64)])
    from_low, from_high = by_rows(pair, along_z(1)), by_rows(pair, along_z(-1))
    up, down = spliced("patch_ends", [(from_low, 0, 64)], [(from_high, 64, 64)])
    last_low, last_high = by_rows(up, along_z(1)), by_rows(down, along_z(-1))
    groups = [pair, from_low, from_high, last_low, last_high]
    pieces = groups + [by_rows(group, SWAP_CORE) for group in groups]
    pieces_layout = [
        layout
        for core in (0, 1)
        for layout in (
            [(0, 64, (0, 0, core), 0), (64, 64, (1, 0, core), 0)],
            [(0, 64, (0, -1, core), 0), (64, 64, (1, -1, core), 0)],
            [(0, 64, (0, 1, core), 0), (64, 64, (1, 1, core), 0)],
            [(0, 64, (0, 2, core), 0)],
            [(0, 64, (1, 2, core), 0)],
        )
    ]

    from_left, from_right = by_frames(folded, along_x(1)), by_frames(folded, along_x(-1))
    across = by_frames(folded, SWAP_Y_HI)
    to_right, to_left = spliced(
        "fold_parts", ((from_left, 0, 96), (across, 0, 192)), ((from_right, 96, 96), (across, 0, 192))
    )
    far_left, far_right = by_frames(to_right, along_x(1)), by_frames(to_left, along_x(-1))
    to_right, to_left = spliced("fold_ends", ((far_left, 96, 96),), ((far_right, 192, 96),))
    last_left, last_right = by_frames(to_right, along_x(1)), by_frames(to_left, along_x(-1))
    weights = [folded, from_left, from_right, across, far_left, far_right]
    weights_layout = [
        [(0, 192, (0, 0), 0)],
        [(0, 192, (0, -1), 0)],
        [(0, 192, (0, 1), 0)],
        [(0, 192, (1, 0), 0)],
        [(0, 96, (0, 2), 0), (96, 192, (1, -1), 0)],
        [(0, 96, (0, 2), 96), (96, 192, (1, 1), 0)],
    ]

    stats, tokens = moments(pieces, pieces_layout, w_embed)
    total = project_most(tokens, weights, weights_layout)
    for pairs, features in ((SWAP_Y_LO, 320), (SWAP_Z, 640), (SWAP_Z_RING, 1280), (SWAP_CORE, 2560)):
        swapped = by_rows(stats, pairs)
        if pairs is SWAP_Z_RING:
            swapped, total = lax.optimization_barrier((swapped, total))
        stats = merged([stats, swapped], features)
    return project_last(tokens, total, last_left, last_right, stats)


def solution(mesh):
    placed = (P("frames", "rows", None, None), P(), P(), P(), P(None, "rows"), P(None, "rows"))
    return jax.shard_map(
        shards,
        mesh=mesh,
        in_specs=placed,
        out_specs=P("frames", None, None, "rows"),
        check_vma=False,
    )
```

time: 778 us -> 88.2 us (0.11)
  waiting for transfers between devices: 466 us -> 19.8 us
  other arithmetic: 149 us -> 0.01 us
  matrix products: 122 us -> 0 us
  Pallas kernels: 0 us -> 24.3 us
  starting transfers between devices: 19.6 us -> 43.6 us
  between operations: 14 us -> 0.38 us
    all_gather x2 -> x0, waiting for transfers between devices: 454 us -> none  [the longest x1 408 us: shards(): embedded = lax.all_gather(embedded, 'rows', axis=3, tiled=True)]
    dot_general x57 -> x0, matrix products: 122 us -> none  [the longest x1 96.7 us: shards(): jnp.einsum('fhwd,de->fhwe', normed, w_qkv, preferred_element_type=jnp.flo...]
    reduce_sum x3 -> x0, other arithmetic: 91.7 us -> none  [the longest x1 45.3 us: shards(): jnp.mean(centred * centred, axis=-1, keepdims=True) + 1e-06]
    convert_element_type x3 -> x0, other arithmetic: 57 us -> none  [the longest x1 55.6 us: shards(): normed = (centred * lax.rsqrt(jnp.mean(centred * centred, axis=-1, keepdi...]
    pallas_call x0 -> x15, Pallas kernels: none -> 24.3 us  [the longest x1 11.2 us: convolutions(): pl.pallas_call(conv_kernel, out_shape=pltpu.VMEM((64, 1536), BF16), in_sp...]
    ppermute x6 -> x32, starting transfers between devices: 19.5 us -> 43.6 us  [the longest x23 27.8 us: by_rows(): return lax.ppermute(x, 'rows', pairs)]
    ppermute x6 -> x32, waiting for transfers between devices: 11.5 us -> 19.8 us  [the longest x23 12.3 us: by_rows(): return lax.ppermute(x, 'rows', pairs)]
  transfers between devices with their start and end apart: 8 -> 32, of which waited for: 7 -> 12; matrix products, arithmetic and copies ran while one was open for 0% -> 0% of each run, Pallas kernels for 0% -> 25%
where the time goes in v2:
time: 88.2 us; the launch traced here: 88 us
  starting transfers between devices  43.6 us (49%)
  Pallas kernels  24.3 us (28%)
  waiting for transfers between devices  19.8 us (22%)
    ppermute x23, starting transfers between devices, by_rows(): return lax.ppermute(x, 'rows', pairs)  27.8 us
    ppermute x8, starting transfers between devices, by_frames(): return lax.ppermute(x, 'frames', pairs)  12.4 us
    ppermute x23, waiting for transfers between devices, by_rows(): return lax.ppermute(x, 'rows', pairs)  12.3 us
    pallas_call x1, Pallas kernels, convolutions(): pl.pallas_call(conv_kernel, out_shape=pltpu.VMEM((64, 1536), BF16), in_sp...  11.2 us
    ppermute x1, waiting for transfers between devices, shards(): back_chip = lax.ppermute(video, ('frames', 'rows'), NEXT_FRAMES_SWAP_CHIP)  6.23 us
    pallas_call x1, Pallas kernels, fold(): pl.pallas_call(fold_kernel, out_shape=pltpu.VMEM((192, 960), BF16), in_sp...  4.33 us
    pallas_call x1, Pallas kernels, project_most(): pl.pallas_call(lambda *refs: most_kernel(layout, *refs), out_shape=pltpu....  3.64 us
    ppermute x1, starting transfers between devices, shards(): back_chip = lax.ppermute(video, ('frames', 'rows'), NEXT_FRAMES_SWAP_CHIP)  3.35 us
  transfers between devices with their start and end apart: 32, of which 12 were waited for; matrix products, arithmetic and copies ran while one was open for 0% of the time, Pallas kernels for 25%

profile of v2, /device:TPU:1, one launch (start us, length us, event | category | flops | bytes accessed | tf_op | source)
XLA Modules:
  0.0 88.0 jit_solution(14366919380838810007)
XLA Ops:
  0.0 2.0 %collective-permute-start.3 = (bf16[4,2,32,192]{3,2,1,0:T(8,128)(2,1)}, bf16[4,2,32,192]{3,2,1,0:T(8,128)(2,1)S(1)}, u32[]{:S(2)}, u32[]{:S(2)}) collective-permute-start(bf16[4,2,32,192]{3,2,1,0:T(8,128)(2,1)} %video.1), channel_id=1, source_target_pairs={{0,16},{16,32},{32,48},{48,64},{64,80},{80,96},{96,112},{112,0},{1... | collective-permute-start | bytes 294920 | tf_op jit(solution)/shard_map/ppermute | solution.py:42
  2.0 1.1 %embed_slice.1.refs_0_ = bf16[480,128]{1,0:T(8,128)(2,1)S(1)} custom-call(bf16[320,1536]{1,0:T(8,128)(2,1)} %bitcast.4), custom_call_target="tpu_custom_call" | custom-call | flops 1000000 | bytes 1000000 | tf_op jit(solution)/shard_map/embed_slice/pallas_call | solution.py:397
  3.2 1.7 %collective-permute-start = (bf16[480,128]{1,0:T(8,128)(2,1)S(1)}, bf16[480,128]{1,0:T(8,128)(2,1)S(1)}, u32[]{:S(2)}, u32[]{:S(2)}) collective-permute-start(bf16[480,128]{1,0:T(8,128)(2,1)S(1)} %embed_slice.1.refs_0_), channel_id=1, source_target_pairs={{0,2},{1,3},{2,4},{3,5},{4,6},{5,7},{6,0},{7,1},{8,10},{9,11},{10,... | collective-permute-start | bytes 368648 | tf_op jit(solution)/shard_map/ppermute | solution.py:38
  4.9 2.2 %collective-permute-start.1 = (bf16[480,128]{1,0:T(8,128)(2,1)S(1)}, bf16[480,128]{1,0:T(8,128)(2,1)S(1)}, u32[]{:S(2)}, u32[]{:S(2)}) collective-permute-start(bf16[480,128]{1,0:T(8,128)(2,1)S(1)} %embed_slice.1.refs_0_), channel_id=1, source_target_pairs={{0,6},{1,7},{2,0},{3,1},{4,2},{5,3},{6,4},{7,5},{8,14},{9,15},{10,... | collective-permute-start | bytes 368648 | tf_op jit(solution)/shard_map/ppermute | solution.py:38
  7.1 1.2 %collective-permute-start.2 = (bf16[480,128]{1,0:T(8,128)(2,1)S(1)}, bf16[480,128]{1,0:T(8,128)(2,1)S(1)}, u32[]{:S(2)}, u32[]{:S(2)}) collective-permute-start(bf16[480,128]{1,0:T(8,128)(2,1)S(1)} %embed_slice.1.refs_0_), channel_id=1, source_target_pairs={{0,4},{1,5},{2,6},{3,7},{4,0},{5,1},{6,2},{7,3},{8,12},{9,13},{10,... | collective-permute-start | bytes 368648 | tf_op jit(solution)/shard_map/ppermute | solution.py:38
  8.3 3.3 %collective-permute-start.4 = (bf16[4,2,32,192]{3,2,1,0:T(8,128)(2,1)}, bf16[4,2,32,192]{3,2,1,0:T(8,128)(2,1)S(1)}, u32[]{:S(2)}, u32[]{:S(2)}) collective-permute-start(bf16[4,2,32,192]{3,2,1,0:T(8,128)(2,1)} %video.1), channel_id=1, source_target_pairs={{0,31},{1,18},{2,17},{3,20},{4,19},{5,22},{6,21},{7,24},{8,23},{9,... | collective-permute-start | bytes 294920 | tf_op jit(solution)/shard_map/ppermute | solution.py:410
  11.6 0.0 collective-permute-done.3.back
  11.6 0.5 collective-permute-start.5
  12.1 6.2 %collective-permute-done.4.back_chip = bf16[4,2,32,192]{3,2,1,0:T(8,128)(2,1)S(1)} collective-permute-done((bf16[4,2,32,192]{3,2,1,0:T(8,128)(2,1)}, bf16[4,2,32,192]{3,2,1,0:T(8,128)(2,1)S(1)}, u32[]{:S(2)}, u32[]{:S(2)}) %collective-permute-start.4) | collective-permute-done | bytes 98336 | tf_op jit(solution)/shard_map/ppermute | solution.py:410
  18.4 2.4 %collective-permute-start.7 = (bf16[4,2,32,192]{3,2,1,0:T(8,128)(2,1)}, bf16[4,2,32,192]{3,2,1,0:T(8,128)(2,1)S(1)}, u32[]{:S(2)}, u32[]{:S(2)}) collective-permute-start(bf16[4,2,32,192]{3,2,1,0:T(8,128)(2,1)} %video.1), channel_id=1, source_target_pairs={{0,1},{1,0},{2,3},{3,2},{4,5},{5,4},{6,7},{7,6},{8,9},{9,8},{10,11... | collective-permute-start | bytes 294920 | tf_op jit(solution)/shard_map/ppermute | solution.py:38
  20.8 0.0 collective-permute-done.2.refs_3_
  20.8 0.1 collective-permute-start.8
  20.9 0.0 slice-start
  21.0 0.4 collective-permute-start.6
  21.4 0.8 collective-permute-start.10
  22.2 0.0 collective-permute-done.7.side_core
  22.2 0.1 collective-permute-done.8.back_core
  22.2 11.2 %convolutions.1.refs_0_ = bf16[64,1536]{1,0:T(8,128)(2,1)S(1)} custom-call(bf16[4,2,32,192]{3,2,1,0:T(8,128)(2,1)S(1)} %collective-permute-done.7.side_core, bf16[4,2,32,192]{3,2,1,0:T(8,128)(2,1)S(1)} %collective-permute-done.5.side_chip, bf16[4,2,32,192]{3,2,1,0:T(8,128)(2,1)S(1)} %collective-permute-done.3.back, ...), custom_call_target="tpu_custom_call" | custom-call | flops 8000000000 | bytes 13000000 | tf_op jit(solution)/shard_map/convolutions/pallas_call | solution.py:177
  33.5 0.0 collective-permute-done.6.refs_1_
  33.5 1.2 %collective-permute-start.11 = (bf16[1920,128]{1,0:T(8,128)(2,1)S(1)}, bf16[1920,128]{1,0:T(8,128)(2,1)S(1)}, u32[]{:S(2)}, u32[]{:S(2)}) collective-permute-start(bf16[1920,128]{1,0:T(8,128)(2,1)S(1)} %collective-permute-done.6.refs_1_), channel_id=1, source_target_pairs={{0,1},{1,0},{2,3},{3,2},{4,5},{5,4},{6,7},{7,6},{8,9},{9,8},{10,11... | collective-permute-start | bytes 1474568 | tf_op jit(solution)/shard_map/ppermute | solution.py:38
  34.7 0.4 collective-permute-start.9
  35.0 1.1 %collective-permute-done.11.refs_3_ = bf16[1920,128]{1,0:T(8,128)(2,1)S(1)} collective-permute-done((bf16[1920,128]{1,0:T(8,128)(2,1)S(1)}, bf16[1920,128]{1,0:T(8,128)(2,1)S(1)}, u32[]{:S(2)}, u32[]{:S(2)}) %collective-permute-start.11) | collective-permute-done | bytes 491552 | tf_op jit(solution)/shard_map/ppermute | solution.py:38
  36.2 0.0 copy-start
  36.2 4.3 %fold.1.refs_1_ = bf16[192,960]{1,0:T(8,128)(2,1)S(1)} custom-call(bf16[1920,128]{1,0:T(8,128)(2,1)S(1)} %embed_four.1.refs_0_, bf16[1920,128]{1,0:T(8,128)(2,1)S(1)} %collective-permute-done.6.refs_1_, bf16[1920,128]{1,0:T(8,128)(2,1)S(1)} %collective-permute-done.10.refs_2_, bf16[1920,128]{1,0:T(8,128)(2,1)S(1)} %collective-permute-done.11.refs_3_, ...), custom_call_target="tpu_custom_call" | custom-call | flops 4000000000 | bytes 12000000 | tf_op jit(solution)/shard_map/fold/pallas_call | solution.py:228
  40.5 0.7 collective-permute-done.9.refs_1_
  41.2 0.1 collective-permute-start.12
  41.3 2.7 %collective-permute-start.13 = (bf16[128,1536]{1,0:T(8,128)(2,1)S(1)}, bf16[128,1536]{1,0:T(8,128)(2,1)S(1)}, u32[]{:S(2)}, u32[]{:S(2)}) collective-permute-start(bf16[128,1536]{1,0:T(8,128)(2,1)S(1)} %patch_pair.1.refs_0_), channel_id=1, source_target_pairs={{0,6},{1,7},{2,0},{3,1},{4,2},{5,3},{6,4},{7,5},{8,14},{9,15},{10,... | collective-permute-start | bytes 1179656 | tf_op jit(solution)/shard_map/ppermute | solution.py:38
  44.0 2.7 %collective-permute-start.25 = (bf16[192,960]{1,0:T(8,128)(2,1)S(1)}, bf16[192,960]{1,0:T(8,128)(2,1)S(1)}, u32[]{:S(2)}, u32[]{:S(2)}) collective-permute-start(bf16[192,960]{1,0:T(8,128)(2,1)S(1)} %fold.1.refs_1_), channel_id=1, source_target_pairs={{0,48},{16,0},{32,16},{48,32},{64,112},{80,64},{96,80},{112,96},{1... | collective-permute-start | bytes 1105928 | tf_op jit(solution)/shard_map/ppermute | solution.py:42
  46.7 2.3 %collective-permute-start.26 = (bf16[192,960]{1,0:T(8,128)(2,1)S(1)}, bf16[192,960]{1,0:T(8,128)(2,1)S(1)}, u32[]{:S(2)}, u32[]{:S(2)}) collective-permute-start(bf16[192,960]{1,0:T(8,128)(2,1)S(1)} %fold.1.refs_1_), channel_id=1, source_target_pairs={{0,64},{16,80},{32,96},{48,112},{64,0},{80,16},{96,32},{112,48},{1... | collective-permute-start | bytes 1105928 | tf_op jit(solution)/shard_map/ppermute | solution.py:42
  48.9 3.4 %collective-permute-done.12.refs_0_.refs_1_ = bf16[128,1536]{1,0:T(8,128)(2,1)S(1)} collective-permute-done((bf16[128,1536]{1,0:T(8,128)(2,1)S(1)}, bf16[128,1536]{1,0:T(8,128)(2,1)S(1)}, u32[]{:S(2)}, u32[]{:S(2)}) %collective-permute-start.12) | collective-permute-done | bytes 393248 | tf_op jit(solution)/shard_map/ppermute | solution.py:38
  52.4 1.7 %collective-permute-start.16 = (bf16[128,1536]{1,0:T(8,128)(2,1)S(1)}, bf16[128,1536]{1,0:T(8,128)(2,1)S(1)}, u32[]{:S(2)}, u32[]{:S(2)}) collective-permute-start(bf16[128,1536]{1,0:T(8,128)(2,1)S(1)} %patch_pair.1.refs_0_), channel_id=1, source_target_pairs={{0,1},{1,0},{2,3},{3,2},{4,5},{5,4},{6,7},{7,6},{8,9},{9,8},{10,11... | collective-permute-start | bytes 1179656 | tf_op jit(solution)/shard_map/ppermute | solution.py:38
  54.0 0.0 collective-permute-done.13.refs_1_.refs_2_
  54.1 0.0 collective-permute-start.17
  54.1 0.4 collective-permute-done.24.refs_0_.refs_2_
  54.5 0.0 collective-permute-start.14
  54.5 0.0 collective-permute-done.25.refs_2_.refs_3_
  54.5 2.7 %collective-permute-start.15 = (bf16[64,1536]{1,0:T(8,128)(2,1)S(1)}, bf16[64,1536]{1,0:T(8,128)(2,1)S(1)}, u32[]{:S(2)}, u32[]{:S(2)}) collective-permute-start(bf16[64,1536]{1,0:T(8,128)(2,1)S(1)} %get-tuple-element.35), channel_id=1, source_target_pairs={{0,6},{1,7},{2,0},{3,1},{4,2},{5,3},{6,4},{7,5},{8,14},{9,15},{10,... | collective-permute-start | bytes 589832 | tf_op jit(solution)/shard_map/ppermute | solution.py:38
  57.1 2.8 %collective-permute-start.18 = (bf16[128,1536]{1,0:T(8,128)(2,1)S(1)}, bf16[128,1536]{1,0:T(8,128)(2,1)S(1)}, u32[]{:S(2)}, u32[]{:S(2)}) collective-permute-start(bf16[128,1536]{1,0:T(8,128)(2,1)S(1)} %collective-permute-done.13.refs_1_.refs_2_), channel_id=1, source_target_pairs={{0,1},{1,0},{2,3},{3,2},{4,5},{5,4},{6,7},{7,6},{8,9},{9,8},{10,11... | collective-permute-start | bytes 1179656 | tf_op jit(solution)/shard_map/ppermute | solution.py:38
  60.0 0.1 fold_parts.1
  60.1 0.0 collective-permute-done.16.refs_5_
  60.1 0.1 collective-permute-start.27
  60.1 0.0 collective-permute-done.14.refs_3_
  60.2 2.6 %collective-permute-start.28 = (bf16[288,960]{1,0:T(8,128)(2,1)S(1)}, bf16[288,960]{1,0:T(8,128)(2,1)S(1)}, u32[]{:S(2)}, u32[]{:S(2)}) collective-permute-start(bf16[288,960]{1,0:T(8,128)(2,1)S(1)} %get-tuple-element.40), channel_id=1, source_target_pairs={{0,48},{16,0},{32,16},{48,32},{64,112},{80,64},{96,80},{112,96},{1... | collective-permute-start | bytes 1658888 | tf_op jit(solution)/shard_map/ppermute | solution.py:42
  62.8 0.0 collective-permute-done.15.refs_4_
  62.8 2.2 %collective-permute-start.19 = (bf16[64,1536]{1,0:T(8,128)(2,1)S(1)}, bf16[64,1536]{1,0:T(8,128)(2,1)S(1)}, u32[]{:S(2)}, u32[]{:S(2)}) collective-permute-start(bf16[64,1536]{1,0:T(8,128)(2,1)S(1)} %collective-permute-done.14.refs_3_), channel_id=1, source_target_pairs={{0,1},{1,0},{2,3},{3,2},{4,5},{5,4},{6,7},{7,6},{8,9},{9,8},{10,11... | collective-permute-start | bytes 589832 | tf_op jit(solution)/shard_map/ppermute | solution.py:38
  65.0 0.1 collective-permute-start.20
  65.1 1.0 %collective-permute-done.19.refs_8_ = bf16[64,1536]{1,0:T(8,128)(2,1)S(1)} collective-permute-done((bf16[64,1536]{1,0:T(8,128)(2,1)S(1)}, bf16[64,1536]{1,0:T(8,128)(2,1)S(1)}, u32[]{:S(2)}, u32[]{:S(2)}) %collective-permute-start.19) | collective-permute-done | bytes 196640 | tf_op jit(solution)/shard_map/ppermute | solution.py:38
  66.0 0.4 collective-permute-done.20.refs_9_
  66.4 1.6 %moments.1 = (f32[8,256]{1,0:T(8,128)S(1)}, bf16[16,64,1536]{2,1,0:T(8,128)(2,1)S(1)}) custom-call(bf16[128,1536]{1,0:T(8,128)(2,1)S(1)} %patch_pair.1.refs_0_, bf16[128,1536]{1,0:T(8,128)(2,1)S(1)} %collective-permute-done.12.refs_0_.refs_1_, bf16[128,1536]{1,0:T(8,128)(2,1)S(1)} %collective-permute-done.13.refs_1_.refs_2_, ...), custom_call_target="tpu_custom_call" | custom-call | flops 2000000000 | bytes 5000000 | tf_op jit(solution)/shard_map/moments/pallas_call | solution.py:260
  68.0 0.9 %collective-permute-start.21 = (f32[8,256]{1,0:T(8,128)S(1)}, f32[8,256]{1,0:T(8,128)S(1)}, u32[]{:S(2)}, u32[]{:S(2)}) collective-permute-start(f32[8,256]{1,0:T(8,128)S(1)} %get-tuple-element.37.refs_0_), channel_id=1, source_target_pairs={{0,8},{1,9},{2,10},{3,11},{4,12},{5,13},{6,14},{7,15},{8,0},{9,1},... | collective-permute-start | bytes 24584 | tf_op jit(solution)/shard_map/ppermute | solution.py:38
  68.9 1.9 %collective-permute-done.21.refs_1_ = f32[8,256]{1,0:T(8,128)S(1)} collective-permute-done((f32[8,256]{1,0:T(8,128)S(1)}, f32[8,256]{1,0:T(8,128)S(1)}, u32[]{:S(2)}, u32[]{:S(2)}) %collective-permute-start.21) | collective-permute-done | bytes 8224 | tf_op jit(solution)/shard_map/ppermute | solution.py:38
  70.9 0.1 collective-permute-start.22
  71.0 2.8 %collective-permute-done.22.refs_1_ = f32[8,256]{1,0:T(8,128)S(1)} collective-permute-done((f32[8,256]{1,0:T(8,128)S(1)}, f32[8,256]{1,0:T(8,128)S(1)}, u32[]{:S(2)}, u32[]{:S(2)}) %collective-permute-start.22) | collective-permute-done | bytes 8224 | tf_op jit(solution)/shard_map/ppermute | solution.py:38
  73.8 1.7 %collective-permute-start.23 = (f32[8,256]{1,0:T(8,128)S(1)}, f32[8,256]{1,0:T(8,128)S(1)}, u32[]{:S(2)}, u32[]{:S(2)}) collective-permute-start(f32[8,256]{1,0:T(8,128)S(1)} %merge.5.refs_0_), channel_id=1, source_target_pairs={{0,6},{1,7},{2,4},{3,5},{4,2},{5,3},{6,0},{7,1},{8,14},{9,15},{10,... | collective-permute-start | bytes 24584 | tf_op jit(solution)/shard_map/ppermute | solution.py:38
  75.4 0.9 collective-permute-done.27.refs_5_.refs_0_
  76.3 0.1 collective-permute-start.29
  76.4 2.7 %collective-permute-start.30 = (bf16[96,960]{1,0:T(8,128)(2,1)S(1)}, bf16[96,960]{1,0:T(8,128)(2,1)S(1)}, u32[]{:S(2)}, u32[]{:S(2)}) collective-permute-start(bf16[96,960]{1,0:T(8,128)(2,1)S(1)} %get-tuple-element.43), channel_id=1, source_target_pairs={{0,48},{16,0},{32,16},{48,32},{64,112},{80,64},{96,80},{112,96},{1... | collective-permute-start | bytes 552968 | tf_op jit(solution)/shard_map/ppermute | solution.py:42
  79.1 3.6 %project_most.1.total = f32[1024,960]{1,0:T(8,128)S(1)} custom-call(bf16[16,64,1536]{2,1,0:T(8,128)(2,1)S(1)} %get-tuple-element.36.refs_0_.tokens, bf16[192,960]{1,0:T(8,128)(2,1)S(1)} %fold.1.refs_1_, bf16[192,960]{1,0:T(8,128)(2,1)S(1)} %collective-permute-done.24.refs_0_.refs_2_, bf16[192,960]{1,0:T(8,128)(2,1)S(1)} %collective-permute-done.25.refs_2_.refs_3_, ...), custom_call_target="tpu_custom_call" | custom-call | flops 4000000000 | bytes 8000000 | tf_op jit(solution)/shard_map/project_most/pallas_call | solution.py:306
  82.7 0.0 collective-permute-done.23.refs_1_
  82.8 2.0 %collective-permute-start.31 = (f32[8,256]{1,0:T(8,128)S(1)}, f32[8,256]{1,0:T(8,128)S(1)}, u32[]{:S(2)}, u32[]{:S(2)}) collective-permute-start(f32[8,256]{1,0:T(8,128)S(1)} %merge.6.refs_0_), channel_id=1, source_target_pairs={{0,1},{1,0},{2,3},{3,2},{4,5},{5,4},{6,7},{7,6},{8,9},{9,8},{10,11... | collective-permute-start | bytes 24584 | tf_op jit(solution)/shard_map/ppermute | solution.py:38
  84.8 0.8 collective-permute-done.31.refs_1_
  85.6 0.0 collective-permute-done.29.low
  85.7 0.0 collective-permute-done.30.high
  85.7 2.2 %project_last.1 = bf16[4,16,16,960]{3,2,1,0:T(8,128)(2,1)} custom-call(bf16[16,64,1536]{2,1,0:T(8,128)(2,1)S(1)} %get-tuple-element.36.refs_0_.tokens, f32[1024,960]{1,0:T(8,128)S(1)} %project_most.1.total, bf16[96,960]{1,0:T(8,128)(2,1)S(1)} %collective-permute-done.29.low, bf16[96,960]{1,0:T(8,128)(2,1)S(1)} %collective-permute-done.30.high, ...), custom_call_target="tpu_custom_call" | custom-call | flops 2000000000 | bytes 8000000 | tf_op jit(solution)/shard_map/project_last/pallas_call | solution.py:343
  (24 shorter events, 0.2 us)
Async XLA Ops:
  0.0 11.6 %collective-permute-start.3 = (bf16[4,2,32,192]{3,2,1,0:T(8,128)(2,1)}, bf16[4,2,32,192]{3,2,1,0:T(8,128)(2,1)S(1)}, u32[]{:S(2)}, u32[]{:S(2)}) collective-permute-start(bf16[4,2,32,192]{3,2,1,0:T(8,128)(2,1)} %video.1), channel_id=1, source_target_pairs={{0,16},{16,32},{32,48},{48,64},{64,80},{80,96},{96,112},{112,0},{1... | collective-permute-start | bytes 294920 | tf_op jit(solution)/shard_map/ppermute | solution.py:42
  3.2 17.6 %collective-permute-start = (bf16[480,128]{1,0:T(8,128)(2,1)S(1)}, bf16[480,128]{1,0:T(8,128)(2,1)S(1)}, u32[]{:S(2)}, u32[]{:S(2)}) collective-permute-start(bf16[480,128]{1,0:T(8,128)(2,1)S(1)} %embed_slice.1.refs_0_), channel_id=1, source_target_pairs={{0,2},{1,3},{2,4},{3,5},{4,6},{5,7},{6,0},{7,1},{8,10},{9,11},{10,... | collective-permute-start | bytes 368648 | tf_op jit(solution)/shard_map/ppermute | solution.py:38
  4.9 15.9 %collective-permute-start.1 = (bf16[480,128]{1,0:T(8,128)(2,1)S(1)}, bf16[480,128]{1,0:T(8,128)(2,1)S(1)}, u32[]{:S(2)}, u32[]{:S(2)}) collective-permute-start(bf16[480,128]{1,0:T(8,128)(2,1)S(1)} %embed_slice.1.refs_0_), channel_id=1, source_target_pairs={{0,6},{1,7},{2,0},{3,1},{4,2},{5,3},{6,4},{7,5},{8,14},{9,15},{10,... | collective-permute-start | bytes 368648 | tf_op jit(solution)/shard_map/ppermute | solution.py:38
  7.1 13.7 %collective-permute-start.2 = (bf16[480,128]{1,0:T(8,128)(2,1)S(1)}, bf16[480,128]{1,0:T(8,128)(2,1)S(1)}, u32[]{:S(2)}, u32[]{:S(2)}) collective-permute-start(bf16[480,128]{1,0:T(8,128)(2,1)S(1)} %embed_slice.1.refs_0_), channel_id=1, source_target_pairs={{0,4},{1,5},{2,6},{3,7},{4,0},{5,1},{6,2},{7,3},{8,12},{9,13},{10,... | collective-permute-start | bytes 368648 | tf_op jit(solution)/shard_map/ppermute | solution.py:38
  8.3 10.1 %collective-permute-start.4 = (bf16[4,2,32,192]{3,2,1,0:T(8,128)(2,1)}, bf16[4,2,32,192]{3,2,1,0:T(8,128)(2,1)S(1)}, u32[]{:S(2)}, u32[]{:S(2)}) collective-permute-start(bf16[4,2,32,192]{3,2,1,0:T(8,128)(2,1)} %video.1), channel_id=1, source_target_pairs={{0,31},{1,18},{2,17},{3,20},{4,19},{5,22},{6,21},{7,24},{8,23},{9,... | collective-permute-start | bytes 294920 | tf_op jit(solution)/shard_map/ppermute | solution.py:410
  11.6 9.1 %collective-permute-start.5 = (bf16[4,2,32,192]{3,2,1,0:T(8,128)(2,1)}, bf16[4,2,32,192]{3,2,1,0:T(8,128)(2,1)S(1)}, u32[]{:S(2)}, u32[]{:S(2)}) collective-permute-start(bf16[4,2,32,192]{3,2,1,0:T(8,128)(2,1)} %video.1), channel_id=1, source_target_pairs={{0,15},{1,2},{2,1},{3,4},{4,3},{5,6},{6,5},{7,8},{8,7},{9,10},{10,... | collective-permute-start | bytes 294920 | tf_op jit(solution)/shard_map/ppermute | solution.py:38
  18.4 3.8 %collective-permute-start.7 = (bf16[4,2,32,192]{3,2,1,0:T(8,128)(2,1)}, bf16[4,2,32,192]{3,2,1,0:T(8,128)(2,1)S(1)}, u32[]{:S(2)}, u32[]{:S(2)}) collective-permute-start(bf16[4,2,32,192]{3,2,1,0:T(8,128)(2,1)} %video.1), channel_id=1, source_target_pairs={{0,1},{1,0},{2,3},{3,2},{4,5},{5,4},{6,7},{7,6},{8,9},{9,8},{10,11... | collective-permute-start | bytes 294920 | tf_op jit(solution)/shard_map/ppermute | solution.py:38
  20.8 1.4 %collective-permute-start.8 = (bf16[4,2,32,192]{3,2,1,0:T(8,128)(2,1)S(1)}, bf16[4,2,32,192]{3,2,1,0:T(8,128)(2,1)S(1)}, u32[]{:S(2)}, u32[]{:S(2)}) collective-permute-start(bf16[4,2,32,192]{3,2,1,0:T(8,128)(2,1)S(1)} %collective-permute-done.3.back), channel_id=1, source_target_pairs={{0,1},{1,0},{2,3},{3,2},{4,5},{5,4},{6,7},{7,6},{8,9},{9,8},{10,11... | collective-permute-start | bytes 294920 | tf_op jit(solution)/shard_map/ppermute | solution.py:38
  20.9 15.3 %slice-start = ((s8[9830400]{0:T(1024)(128)(4,1)}), s8[4194304]{0:T(1024)(128)(4,1)S(1)}, s32[]{:S(2)}) async-start(s8[9830400]{0:T(1024)(128)(4,1)} %bitcast.6), calls=%async_computation | async-start | bytes 8388608
  21.0 12.5 %collective-permute-start.6 = (bf16[1920,128]{1,0:T(8,128)(2,1)S(1)}, bf16[1920,128]{1,0:T(8,128)(2,1)S(1)}, u32[]{:S(2)}, u32[]{:S(2)}) collective-permute-start(bf16[1920,128]{1,0:T(8,128)(2,1)S(1)} %embed_four.1.refs_0_), channel_id=1, source_target_pairs={{0,8},{1,9},{2,10},{3,11},{4,12},{5,13},{6,14},{7,15},{8,0},{9,1},... | collective-permute-start | bytes 1474568 | tf_op jit(solution)/shard_map/ppermute | solution.py:38
  21.4 13.6 %collective-permute-start.10 = (bf16[1920,128]{1,0:T(8,128)(2,1)S(1)}, bf16[1920,128]{1,0:T(8,128)(2,1)S(1)}, u32[]{:S(2)}, u32[]{:S(2)}) collective-permute-start(bf16[1920,128]{1,0:T(8,128)(2,1)S(1)} %embed_four.1.refs_0_), channel_id=1, source_target_pairs={{0,1},{1,0},{2,3},{3,2},{4,5},{5,4},{6,7},{7,6},{8,9},{9,8},{10,11... | collective-permute-start | bytes 1474568 | tf_op jit(solution)/shard_map/ppermute | solution.py:38
  22.2 13.9 %slice-start.1 = ((s8[9830400]{0:T(1024)(128)(4,1)}), s8[4194304]{0:T(1024)(128)(4,1)S(1)}, s32[]{:S(2)}) async-start(s8[9830400]{0:T(1024)(128)(4,1)} %bitcast.6), calls=%async_computation.1 | async-start | bytes 8388608
  22.2 13.9 %slice-start.2 = ((s8[9830400]{0:T(1024)(128)(4,1)}), s8[1441792]{0:T(1024)(128)(4,1)S(1)}, s32[]{:S(2)}) async-start(s8[9830400]{0:T(1024)(128)(4,1)} %bitcast.6), calls=%async_computation.2 | async-start | bytes 2883584
  33.5 2.7 %collective-permute-start.11 = (bf16[1920,128]{1,0:T(8,128)(2,1)S(1)}, bf16[1920,128]{1,0:T(8,128)(2,1)S(1)}, u32[]{:S(2)}, u32[]{:S(2)}) collective-permute-start(bf16[1920,128]{1,0:T(8,128)(2,1)S(1)} %collective-permute-done.6.refs_1_), channel_id=1, source_target_pairs={{0,1},{1,0},{2,3},{3,2},{4,5},{5,4},{6,7},{7,6},{8,9},{9,8},{10,11... | collective-permute-start | bytes 1474568 | tf_op jit(solution)/shard_map/ppermute | solution.py:38
  34.7 6.5 %collective-permute-start.9 = (bf16[64,1536]{1,0:T(8,128)(2,1)S(1)}, bf16[64,1536]{1,0:T(8,128)(2,1)S(1)}, u32[]{:S(2)}, u32[]{:S(2)}) collective-permute-start(bf16[64,1536]{1,0:T(8,128)(2,1)S(1)} %convolutions.1.refs_0_), channel_id=1, source_target_pairs={{0,8},{1,9},{2,10},{3,11},{4,12},{5,13},{6,14},{7,15},{8,0},{9,1},... | collective-permute-start | bytes 589832 | tf_op jit(solution)/shard_map/ppermute | solution.py:38
  36.2 30.2 %copy-start = (bf16[1536,320]{0,1:T(8,128)(2,1)S(1)}, bf16[1536,320]{0,1:T(8,128)(2,1)}, u32[]{:S(2)}) copy-start(bf16[1536,320]{0,1:T(8,128)(2,1)} %param.10) | copy-start | bytes 2949124
  41.2 11.1 %collective-permute-start.12 = (bf16[128,1536]{1,0:T(8,128)(2,1)S(1)}, bf16[128,1536]{1,0:T(8,128)(2,1)S(1)}, u32[]{:S(2)}, u32[]{:S(2)}) collective-permute-start(bf16[128,1536]{1,0:T(8,128)(2,1)S(1)} %patch_pair.1.refs_0_), channel_id=1, source_target_pairs={{0,2},{1,3},{2,4},{3,5},{4,6},{5,7},{6,0},{7,1},{8,10},{9,11},{10,... | collective-permute-start | bytes 1179656 | tf_op jit(solution)/shard_map/ppermute | solution.py:38
  41.3 12.7 %collective-permute-start.13 = (bf16[128,1536]{1,0:T(8,128)(2,1)S(1)}, bf16[128,1536]{1,0:T(8,128)(2,1)S(1)}, u32[]{:S(2)}, u32[]{:S(2)}) collective-permute-start(bf16[128,1536]{1,0:T(8,128)(2,1)S(1)} %patch_pair.1.refs_0_), channel_id=1, source_target_pairs={{0,6},{1,7},{2,0},{3,1},{4,2},{5,3},{6,4},{7,5},{8,14},{9,15},{10,... | collective-permute-start | bytes 1179656 | tf_op jit(solution)/shard_map/ppermute | solution.py:38
  44.0 10.5 %collective-permute-start.24 = (bf16[192,960]{1,0:T(8,128)(2,1)S(1)}, bf16[192,960]{1,0:T(8,128)(2,1)S(1)}, u32[]{:S(2)}, u32[]{:S(2)}) collective-permute-start(bf16[192,960]{1,0:T(8,128)(2,1)S(1)} %fold.1.refs_1_), channel_id=1, source_target_pairs={{0,16},{16,32},{32,48},{48,0},{64,80},{80,96},{96,112},{112,64},{1... | collective-permute-start | bytes 1105928 | tf_op jit(solution)/shard_map/ppermute | solution.py:42
  44.0 10.5 %collective-permute-start.25 = (bf16[192,960]{1,0:T(8,128)(2,1)S(1)}, bf16[192,960]{1,0:T(8,128)(2,1)S(1)}, u32[]{:S(2)}, u32[]{:S(2)}) collective-permute-start(bf16[192,960]{1,0:T(8,128)(2,1)S(1)} %fold.1.refs_1_), channel_id=1, source_target_pairs={{0,48},{16,0},{32,16},{48,32},{64,112},{80,64},{96,80},{112,96},{1... | collective-permute-start | bytes 1105928 | tf_op jit(solution)/shard_map/ppermute | solution.py:42
  46.7 10.5 %collective-permute-start.26 = (bf16[192,960]{1,0:T(8,128)(2,1)S(1)}, bf16[192,960]{1,0:T(8,128)(2,1)S(1)}, u32[]{:S(2)}, u32[]{:S(2)}) collective-permute-start(bf16[192,960]{1,0:T(8,128)(2,1)S(1)} %fold.1.refs_1_), channel_id=1, source_target_pairs={{0,64},{16,80},{32,96},{48,112},{64,0},{80,16},{96,32},{112,48},{1... | collective-permute-start | bytes 1105928 | tf_op jit(solution)/shard_map/ppermute | solution.py:42
  52.4 7.7 %collective-permute-start.16 = (bf16[128,1536]{1,0:T(8,128)(2,1)S(1)}, bf16[128,1536]{1,0:T(8,128)(2,1)S(1)}, u32[]{:S(2)}, u32[]{:S(2)}) collective-permute-start(bf16[128,1536]{1,0:T(8,128)(2,1)S(1)} %patch_pair.1.refs_0_), channel_id=1, source_target_pairs={{0,1},{1,0},{2,3},{3,2},{4,5},{5,4},{6,7},{7,6},{8,9},{9,8},{10,11... | collective-permute-start | bytes 1179656 | tf_op jit(solution)/shard_map/ppermute | solution.py:38
  54.1 10.9 %collective-permute-start.17 = (bf16[128,1536]{1,0:T(8,128)(2,1)S(1)}, bf16[128,1536]{1,0:T(8,128)(2,1)S(1)}, u32[]{:S(2)}, u32[]{:S(2)}) collective-permute-start(bf16[128,1536]{1,0:T(8,128)(2,1)S(1)} %collective-permute-done.12.refs_0_.refs_1_), channel_id=1, source_target_pairs={{0,1},{1,0},{2,3},{3,2},{4,5},{5,4},{6,7},{7,6},{8,9},{9,8},{10,11... | collective-permute-start | bytes 1179656 | tf_op jit(solution)/shard_map/ppermute | solution.py:38
  54.5 5.7 %collective-permute-start.14 = (bf16[64,1536]{1,0:T(8,128)(2,1)S(1)}, bf16[64,1536]{1,0:T(8,128)(2,1)S(1)}, u32[]{:S(2)}, u32[]{:S(2)}) collective-permute-start(bf16[64,1536]{1,0:T(8,128)(2,1)S(1)} %get-tuple-element.34), channel_id=1, source_target_pairs={{0,2},{1,3},{2,4},{3,5},{4,6},{5,7},{6,0},{7,1},{8,10},{9,11},{10,... | collective-permute-start | bytes 589832 | tf_op jit(solution)/shard_map/ppermute | solution.py:38
  54.5 8.3 %collective-permute-start.15 = (bf16[64,1536]{1,0:T(8,128)(2,1)S(1)}, bf16[64,1536]{1,0:T(8,128)(2,1)S(1)}, u32[]{:S(2)}, u32[]{:S(2)}) collective-permute-start(bf16[64,1536]{1,0:T(8,128)(2,1)S(1)} %get-tuple-element.35), channel_id=1, source_target_pairs={{0,6},{1,7},{2,0},{3,1},{4,2},{5,3},{6,4},{7,5},{8,14},{9,15},{10,... | collective-permute-start | bytes 589832 | tf_op jit(solution)/shard_map/ppermute | solution.py:38
  57.1 7.9 %collective-permute-start.18 = (bf16[128,1536]{1,0:T(8,128)(2,1)S(1)}, bf16[128,1536]{1,0:T(8,128)(2,1)S(1)}, u32[]{:S(2)}, u32[]{:S(2)}) collective-permute-start(bf16[128,1536]{1,0:T(8,128)(2,1)S(1)} %collective-permute-done.13.refs_1_.refs_2_), channel_id=1, source_target_pairs={{0,1},{1,0},{2,3},{3,2},{4,5},{5,4},{6,7},{7,6},{8,9},{9,8},{10,11... | collective-permute-start | bytes 1179656 | tf_op jit(solution)/shard_map/ppermute | solution.py:38
  60.1 16.2 %collective-permute-start.27 = (bf16[288,960]{1,0:T(8,128)(2,1)S(1)}, bf16[288,960]{1,0:T(8,128)(2,1)S(1)}, u32[]{:S(2)}, u32[]{:S(2)}) collective-permute-start(bf16[288,960]{1,0:T(8,128)(2,1)S(1)} %get-tuple-element.39), channel_id=1, source_target_pairs={{0,16},{16,32},{32,48},{48,0},{64,80},{80,96},{96,112},{112,64},{1... | collective-permute-start | bytes 1658888 | tf_op jit(solution)/shard_map/ppermute | solution.py:42
  60.2 16.1 %collective-permute-start.28 = (bf16[288,960]{1,0:T(8,128)(2,1)S(1)}, bf16[288,960]{1,0:T(8,128)(2,1)S(1)}, u32[]{:S(2)}, u32[]{:S(2)}) collective-permute-start(bf16[288,960]{1,0:T(8,128)(2,1)S(1)} %get-tuple-element.40), channel_id=1, source_target_pairs={{0,48},{16,0},{32,16},{48,32},{64,112},{80,64},{96,80},{112,96},{1... | collective-permute-start | bytes 1658888 | tf_op jit(solution)/shard_map/ppermute | solution.py:42
  62.8 3.2 %collective-permute-start.19 = (bf16[64,1536]{1,0:T(8,128)(2,1)S(1)}, bf16[64,1536]{1,0:T(8,128)(2,1)S(1)}, u32[]{:S(2)}, u32[]{:S(2)}) collective-permute-start(bf16[64,1536]{1,0:T(8,128)(2,1)S(1)} %collective-permute-done.14.refs_3_), channel_id=1, source_target_pairs={{0,1},{1,0},{2,3},{3,2},{4,5},{5,4},{6,7},{7,6},{8,9},{9,8},{10,11... | collective-permute-start | bytes 589832 | tf_op jit(solution)/shard_map/ppermute | solution.py:38
  65.0 1.4 %collective-permute-start.20 = (bf16[64,1536]{1,0:T(8,128)(2,1)S(1)}, bf16[64,1536]{1,0:T(8,128)(2,1)S(1)}, u32[]{:S(2)}, u32[]{:S(2)}) collective-permute-start(bf16[64,1536]{1,0:T(8,128)(2,1)S(1)} %collective-permute-done.15.refs_4_), channel_id=1, source_target_pairs={{0,1},{1,0},{2,3},{3,2},{4,5},{5,4},{6,7},{7,6},{8,9},{9,8},{10,11... | collective-permute-start | bytes 589832 | tf_op jit(solution)/shard_map/ppermute | solution.py:38
  68.0 2.9 %collective-permute-start.21 = (f32[8,256]{1,0:T(8,128)S(1)}, f32[8,256]{1,0:T(8,128)S(1)}, u32[]{:S(2)}, u32[]{:S(2)}) collective-permute-start(f32[8,256]{1,0:T(8,128)S(1)} %get-tuple-element.37.refs_0_), channel_id=1, source_target_pairs={{0,8},{1,9},{2,10},{3,11},{4,12},{5,13},{6,14},{7,15},{8,0},{9,1},... | collective-permute-start | bytes 24584 | tf_op jit(solution)/shard_map/ppermute | solution.py:38
  70.9 2.9 %collective-permute-start.22 = (f32[8,256]{1,0:T(8,128)S(1)}, f32[8,256]{1,0:T(8,128)S(1)}, u32[]{:S(2)}, u32[]{:S(2)}) collective-permute-start(f32[8,256]{1,0:T(8,128)S(1)} %merge.4.refs_0_), channel_id=1, source_target_pairs={{0,2},{1,3},{2,0},{3,1},{4,6},{5,7},{6,4},{7,5},{8,10},{9,11},{10,... | collective-permute-start | bytes 24584 | tf_op jit(solution)/shard_map/ppermute | solution.py:38
  73.8 9.0 %collective-permute-start.23 = (f32[8,256]{1,0:T(8,128)S(1)}, f32[8,256]{1,0:T(8,128)S(1)}, u32[]{:S(2)}, u32[]{:S(2)}) collective-permute-start(f32[8,256]{1,0:T(8,128)S(1)} %merge.5.refs_0_), channel_id=1, source_target_pairs={{0,6},{1,7},{2,4},{3,5},{4,2},{5,3},{6,0},{7,1},{8,14},{9,15},{10,... | collective-permute-start | bytes 24584 | tf_op jit(solution)/shard_map/ppermute | solution.py:38
  76.3 9.3 %collective-permute-start.29 = (bf16[96,960]{1,0:T(8,128)(2,1)S(1)}, bf16[96,960]{1,0:T(8,128)(2,1)S(1)}, u32[]{:S(2)}, u32[]{:S(2)}) collective-permute-start(bf16[96,960]{1,0:T(8,128)(2,1)S(1)} %get-tuple-element.42), channel_id=1, source_target_pairs={{0,16},{16,32},{32,48},{48,0},{64,80},{80,96},{96,112},{112,64},{1... | collective-permute-start | bytes 552968 | tf_op jit(solution)/shard_map/ppermute | solution.py:42
  76.4 9.2 %collective-permute-start.30 = (bf16[96,960]{1,0:T(8,128)(2,1)S(1)}, bf16[96,960]{1,0:T(8,128)(2,1)S(1)}, u32[]{:S(2)}, u32[]{:S(2)}) collective-permute-start(bf16[96,960]{1,0:T(8,128)(2,1)S(1)} %get-tuple-element.43), channel_id=1, source_target_pairs={{0,48},{16,0},{32,16},{48,32},{64,112},{80,64},{96,80},{112,96},{1... | collective-permute-start | bytes 552968 | tf_op jit(solution)/shard_map/ppermute | solution.py:42
  82.8 2.9 %collective-permute-start.31 = (f32[8,256]{1,0:T(8,128)S(1)}, f32[8,256]{1,0:T(8,128)S(1)}, u32[]{:S(2)}, u32[]{:S(2)}) collective-permute-start(f32[8,256]{1,0:T(8,128)S(1)} %merge.6.refs_0_), channel_id=1, source_target_pairs={{0,1},{1,0},{2,3},{3,2},{4,5},{5,4},{6,7},{7,6},{8,9},{9,8},{10,11... | collective-permute-start | bytes 24584 | tf_op jit(solution)/shard_map/ppermute | solution.py:38

commit v3 on v2

--- a/solution.py
+++ b/solution.py
@@ -13,21 +13,16 @@
 ROWS_PAIRS = 16
 
 
-def along_x(by):
-    return [(i, i // 4 * 4 + (i + by) % 4) for i in range(FRAMES_PAIRS)]
+def swap_x(k):
+    return [(i, i ^ k) for i in range(FRAMES_PAIRS)]
+
+
+def swap_z(k):
+    return [(i, i ^ (2 * k)) for i in range(ROWS_PAIRS)]
 
 
 SWAP_Y_HI = [(i, i ^ 4) for i in range(FRAMES_PAIRS)]
 NEXT_FRAMES = [(i, (i + 1) % FRAMES_PAIRS) for i in range(FRAMES_PAIRS)]
-
-
-def along_z(by):
-    return [(i, i // 8 * 8 + (i + 2 * by) % 8) for i in range(ROWS_PAIRS)]
-
-
-SWAP_Z, SWAP_Z_RING = ([(i, i ^ 2) for i in range(ROWS_PAIRS)], [(i, i ^ 6) for i in range(ROWS_PAIRS)])
-
-
 SWAP_Y_LO = [(i, i ^ 8) for i in range(ROWS_PAIRS)]
 SWAP_CORE = [(i, i ^ 1) for i in range(ROWS_PAIRS)]
 SWAP_CHIP = [(i, (i + 1) % ROWS_PAIRS if i % 2 else (i - 1) % ROWS_PAIRS) for i in range(ROWS_PAIRS)]
@@ -48,7 +43,7 @@
 
 def at_chip(place, y_lo, z):
     rows = place[1]
-    return (rows // 8 + y_lo) % 2 * 4 + (rows // 2 + z) % 4
+    return (rows // 8 + y_lo) % 2 * 4 + (rows // 2 % 4 ^ z)
 
 
 def at_rows(place, y_lo, z, core):
@@ -56,7 +51,7 @@
 
 
 def at_frames(place, y_hi, x):
-    return (place[0] // 4 + y_hi) % 2 * 4 + (place[0] + x) % 4
+    return (place[0] // 4 + y_hi) % 2 * 4 + (place[0] % 4 ^ x)
 
 
 def whole(memory=pltpu.VMEM):
@@ -205,7 +200,7 @@
     for same, other in zip(refs[:count], refs[count : 2 * count]):
         for n in range(same.shape[0] // 480):
             s = len(chips)
-            chips.append(at_chip(place, s // 4, (0, -1, 1, 2)[s % 4]))
+            chips.append(at_chip(place, s // 4, (0, 1, 3, 2)[s % 4]))
             for ref, at in ((same, core), (other, 1 - core)):
                 block = ref[480 * n : 480 * (n + 1)]
                 first = pl.multiple_of(640 * s + 320 * at, 32)
@@ -410,7 +405,7 @@
     back_chip = lax.ppermute(video, ("frames", "rows"), NEXT_FRAMES_SWAP_CHIP)
     side_core, side_chip = by_rows(video, SWAP_CORE), by_rows(video, SWAP_CHIP)
     mine = embed_slice(w_embed)
-    along = [by_rows(mine, along_z(by)) for by in (1, -1, 2)]
+    along = [by_rows(mine, swap_z(k)) for k in (1, 3, 2)]
     along, back, back_chip, side_chip = lax.optimization_barrier((along, back, back_chip, side_chip))
     back_core = by_rows(back, SWAP_CORE)
     (four,) = spliced("embed_four", [(mine, 0, 480)] + [(part, 0, 480) for part in along])
@@ -424,46 +419,48 @@
     opposite = by_rows(patches, SWAP_Y_LO)
     opposite, folded = lax.optimization_barrier((opposite, folded))
     (pair,) = spliced("patch_pair", [(patches, 0, 64), (opposite, 0, 64)])
-    from_low, from_high = by_rows(pair, along_z(1)), by_rows(pair, along_z(-1))
+    from_low, from_high = by_rows(pair, swap_z(1)), by_rows(pair, swap_z(3))
+    from_left, from_right = by_frames(folded, swap_x(1)), by_frames(folded, swap_x(3))
+    across = by_frames(folded, SWAP_Y_HI)
+    from_low, from_high, from_left, from_right, across = lax.optimization_barrier(
+        (from_low, from_high, from_left, from_right, across)
+    )
     up, down = spliced("patch_ends", [(from_low, 0, 64)], [(from_high, 64, 64)])
-    last_low, last_high = by_rows(up, along_z(1)), by_rows(down, along_z(-1))
-    groups = [pair, from_low, from_high, last_low, last_high]
+    last_low, last_high = by_rows(up, swap_z(3)), by_rows(down, swap_z(1))
+    (most,) = spliced("patch_most", [(pair, 0, 128), (from_low, 0, 128), (from_high, 0, 128)])
+    groups = [most, last_low, last_high]
     pieces = groups + [by_rows(group, SWAP_CORE) for group in groups]
     pieces_layout = [
         layout
         for core in (0, 1)
         for layout in (
-            [(0, 64, (0, 0, core), 0), (64, 64, (1, 0, core), 0)],
-            [(0, 64, (0, -1, core), 0), (64, 64, (1, -1, core), 0)],
-            [(0, 64, (0, 1, core), 0), (64, 64, (1, 1, core), 0)],
+            [(64 * n, 64, (n % 2, (0, 1, 3)[n // 2], core), 0) for n in range(6)],
             [(0, 64, (0, 2, core), 0)],
             [(0, 64, (1, 2, core), 0)],
         )
     ]
 
-    from_left, from_right = by_frames(folded, along_x(1)), by_frames(folded, along_x(-1))
-    across = by_frames(folded, SWAP_Y_HI)
     to_right, to_left = spliced(
         "fold_parts", ((from_left, 0, 96), (across, 0, 192)), ((from_right, 96, 96), (across, 0, 192))
     )
-    far_left, far_right = by_frames(to_right, along_x(1)), by_frames(to_left, along_x(-1))
+    far_left, far_right = by_frames(to_right, swap_x(3)), by_frames(to_left, swap_x(1))
     to_right, to_left = spliced("fold_ends", ((far_left, 96, 96),), ((far_right, 192, 96),))
-    last_left, last_right = by_frames(to_right, along_x(1)), by_frames(to_left, along_x(-1))
+    last_left, last_right = by_frames(to_right, swap_x(1)), by_frames(to_left, swap_x(3))
     weights = [folded, from_left, from_right, across, far_left, far_right]
     weights_layout = [
         [(0, 192, (0, 0), 0)],
-        [(0, 192, (0, -1), 0)],
         [(0, 192, (0, 1), 0)],
+        [(0, 192, (0, 3), 0)],
         [(0, 192, (1, 0), 0)],
-        [(0, 96, (0, 2), 0), (96, 192, (1, -1), 0)],
+        [(0, 96, (0, 2), 0), (96, 192, (1, 3), 0)],
         [(0, 96, (0, 2), 96), (96, 192, (1, 1), 0)],
     ]
 
     stats, tokens = moments(pieces, pieces_layout, w_embed)
     total = project_most(tokens, weights, weights_layout)
-    for pairs, features in ((SWAP_Y_LO, 320), (SWAP_Z, 640), (SWAP_Z_RING, 1280), (SWAP_CORE, 2560)):
+    for pairs, features in ((SWAP_Y_LO, 320), (swap_z(1), 640), (swap_z(3), 1280), (SWAP_CORE, 2560)):
         swapped = by_rows(stats, pairs)
-        if pairs is SWAP_Z_RING:
+        if features == 1280:
             swapped, total = lax.optimization_barrier((swapped, total))
         stats = merged([stats, swapped], features)
     return project_last(tokens, total, last_left, last_right, stats)

time: 88.2 us -> 87.8 us (level)
  starting transfers between devices: 43.6 us -> 34.7 us
  waiting for transfers between devices: 19.8 us -> 28.3 us
    ppermute x8, waiting for transfers between devices: 1.26 us -> 11.3 us  [by_frames(): return lax.ppermute(x, 'frames', pairs)]
    ppermute x8, starting transfers between devices: 12.4 us -> 8.16 us  [by_frames(): return lax.ppermute(x, 'frames', pairs)]
    ppermute x23 -> x21, starting transfers between devices: 27.8 us -> 23.9 us  [by_rows(): return lax.ppermute(x, 'rows', pairs)]
    ppermute x1, waiting for transfers between devices: 6.23 us -> 5.33 us  [shards(): back_chip = lax.ppermute(video, ('frames', 'rows'), NEXT_FRAMES_SWAP_CHIP)]
    ppermute x23 -> x21, waiting for transfers between devices: 12.3 us -> 11.7 us  [by_rows(): return lax.ppermute(x, 'rows', pairs)]
  transfers between devices with their start and end apart: 32 -> 30, of which waited for: 12 -> 14; matrix products, arithmetic and copies ran while one was open for 0% -> 0% of each run, Pallas kernels for 25% -> 25%
where the time goes in v3:
time: 87.8 us; the launch traced here: 87.7 us
  starting transfers between devices  34.7 us (40%)
  waiting for transfers between devices  28.3 us (32%)
  Pallas kernels  24.4 us (28%)
    ppermute x21, starting transfers between devices, by_rows(): return lax.ppermute(x, 'rows', pairs)  23.9 us
    ppermute x21, waiting for transfers between devices, by_rows(): return lax.ppermute(x, 'rows', pairs)  11.7 us
    ppermute x8, waiting for transfers between devices, by_frames(): return lax.ppermute(x, 'frames', pairs)  11.3 us
    pallas_call x1, Pallas kernels, convolutions(): pl.pallas_call(conv_kernel, out_shape=pltpu.VMEM((64, 1536), BF16), in_sp...  11.2 us
    ppermute x8, starting transfers between devices, by_frames(): return lax.ppermute(x, 'frames', pairs)  8.16 us
    ppermute x1, waiting for transfers between devices, shards(): back_chip = lax.ppermute(video, ('frames', 'rows'), NEXT_FRAMES_SWAP_CHIP)  5.33 us
    pallas_call x1, Pallas kernels, fold(): pl.pallas_call(fold_kernel, out_shape=pltpu.VMEM((192, 960), BF16), in_sp...  4.34 us
    pallas_call x1, Pallas kernels, project_most(): pl.pallas_call(lambda *refs: most_kernel(layout, *refs), out_shape=pltpu....  3.64 us
  transfers between devices with their start and end apart: 30, of which 14 were waited for; matrix products, arithmetic and copies ran while one was open for 0% of the time, Pallas kernels for 25%

profile of v3, /device:TPU:1, one launch (start us, length us, event | category | flops | bytes accessed | tf_op | source)
XLA Modules:
  0.0 87.7 jit_solution(8931788821763603667)
XLA Ops:
  0.0 2.0 %collective-permute-start.3 = (bf16[4,2,32,192]{3,2,1,0:T(8,128)(2,1)}, bf16[4,2,32,192]{3,2,1,0:T(8,128)(2,1)S(1)}, u32[]{:S(2)}, u32[]{:S(2)}) collective-permute-start(bf16[4,2,32,192]{3,2,1,0:T(8,128)(2,1)} %video.1), channel_id=1, source_target_pairs={{0,16},{16,32},{32,48},{48,64},{64,80},{80,96},{96,112},{112,0},{1... | collective-permute-start | bytes 294920 | tf_op jit(solution)/shard_map/ppermute | solution.py:37
  2.0 1.1 %embed_slice.1.refs_0_ = bf16[480,128]{1,0:T(8,128)(2,1)S(1)} custom-call(bf16[320,1536]{1,0:T(8,128)(2,1)} %bitcast.4), custom_call_target="tpu_custom_call" | custom-call | flops 1000000 | bytes 1000000 | tf_op jit(solution)/shard_map/embed_slice/pallas_call | solution.py:392
  3.2 1.7 %collective-permute-start = (bf16[480,128]{1,0:T(8,128)(2,1)S(1)}, bf16[480,128]{1,0:T(8,128)(2,1)S(1)}, u32[]{:S(2)}, u32[]{:S(2)}) collective-permute-start(bf16[480,128]{1,0:T(8,128)(2,1)S(1)} %embed_slice.1.refs_0_), channel_id=1, source_target_pairs={{0,2},{1,3},{2,0},{3,1},{4,6},{5,7},{6,4},{7,5},{8,10},{9,11},{10,... | collective-permute-start | bytes 368648 | tf_op jit(solution)/shard_map/ppermute | solution.py:33
  4.9 2.2 %collective-permute-start.1 = (bf16[480,128]{1,0:T(8,128)(2,1)S(1)}, bf16[480,128]{1,0:T(8,128)(2,1)S(1)}, u32[]{:S(2)}, u32[]{:S(2)}) collective-permute-start(bf16[480,128]{1,0:T(8,128)(2,1)S(1)} %embed_slice.1.refs_0_), channel_id=1, source_target_pairs={{0,6},{1,7},{2,4},{3,5},{4,2},{5,3},{6,0},{7,1},{8,14},{9,15},{10,... | collective-permute-start | bytes 368648 | tf_op jit(solution)/shard_map/ppermute | solution.py:33
  7.1 1.1 %collective-permute-start.2 = (bf16[480,128]{1,0:T(8,128)(2,1)S(1)}, bf16[480,128]{1,0:T(8,128)(2,1)S(1)}, u32[]{:S(2)}, u32[]{:S(2)}) collective-permute-start(bf16[480,128]{1,0:T(8,128)(2,1)S(1)} %embed_slice.1.refs_0_), channel_id=1, source_target_pairs={{0,4},{1,5},{2,6},{3,7},{4,0},{5,1},{6,2},{7,3},{8,12},{9,13},{10,... | collective-permute-start | bytes 368648 | tf_op jit(solution)/shard_map/ppermute | solution.py:33
  8.2 2.6 %collective-permute-start.4 = (bf16[4,2,32,192]{3,2,1,0:T(8,128)(2,1)}, bf16[4,2,32,192]{3,2,1,0:T(8,128)(2,1)S(1)}, u32[]{:S(2)}, u32[]{:S(2)}) collective-permute-start(bf16[4,2,32,192]{3,2,1,0:T(8,128)(2,1)} %video.1), channel_id=1, source_target_pairs={{0,31},{1,18},{2,17},{3,20},{4,19},{5,22},{6,21},{7,24},{8,23},{9,... | collective-permute-start | bytes 294920 | tf_op jit(solution)/shard_map/ppermute | solution.py:405
  10.7 0.0 collective-permute-done.3.back
  10.7 1.4 %collective-permute-start.5 = (bf16[4,2,32,192]{3,2,1,0:T(8,128)(2,1)}, bf16[4,2,32,192]{3,2,1,0:T(8,128)(2,1)S(1)}, u32[]{:S(2)}, u32[]{:S(2)}) collective-permute-start(bf16[4,2,32,192]{3,2,1,0:T(8,128)(2,1)} %video.1), channel_id=1, source_target_pairs={{0,15},{1,2},{2,1},{3,4},{4,3},{5,6},{6,5},{7,8},{8,7},{9,10},{10,... | collective-permute-start | bytes 294920 | tf_op jit(solution)/shard_map/ppermute | solution.py:33
  12.1 5.3 %collective-permute-done.4.back_chip = bf16[4,2,32,192]{3,2,1,0:T(8,128)(2,1)S(1)} collective-permute-done((bf16[4,2,32,192]{3,2,1,0:T(8,128)(2,1)}, bf16[4,2,32,192]{3,2,1,0:T(8,128)(2,1)S(1)}, u32[]{:S(2)}, u32[]{:S(2)}) %collective-permute-start.4) | collective-permute-done | bytes 98336 | tf_op jit(solution)/shard_map/ppermute | solution.py:405
  17.4 3.6 %collective-permute-start.7 = (bf16[4,2,32,192]{3,2,1,0:T(8,128)(2,1)}, bf16[4,2,32,192]{3,2,1,0:T(8,128)(2,1)S(1)}, u32[]{:S(2)}, u32[]{:S(2)}) collective-permute-start(bf16[4,2,32,192]{3,2,1,0:T(8,128)(2,1)} %video.1), channel_id=1, source_target_pairs={{0,1},{1,0},{2,3},{3,2},{4,5},{5,4},{6,7},{7,6},{8,9},{9,8},{10,11... | collective-permute-start | bytes 294920 | tf_op jit(solution)/shard_map/ppermute | solution.py:33
  21.1 0.0 collective-permute-done.2.refs_3_
  21.1 0.1 collective-permute-start.8
  21.2 0.0 slice-start
  21.3 0.1 collective-permute-start.6
  21.3 0.6 collective-permute-start.10
  21.9 0.4 collective-permute-done.7.side_core
  22.3 0.3 collective-permute-done.8.back_core
  22.5 11.2 %convolutions.1.refs_0_ = bf16[64,1536]{1,0:T(8,128)(2,1)S(1)} custom-call(bf16[4,2,32,192]{3,2,1,0:T(8,128)(2,1)S(1)} %collective-permute-done.7.side_core, bf16[4,2,32,192]{3,2,1,0:T(8,128)(2,1)S(1)} %collective-permute-done.5.side_chip, bf16[4,2,32,192]{3,2,1,0:T(8,128)(2,1)S(1)} %collective-permute-done.3.back, ...), custom_call_target="tpu_custom_call" | custom-call | flops 8000000000 | bytes 13000000 | tf_op jit(solution)/shard_map/convolutions/pallas_call | solution.py:172
  33.8 0.0 collective-permute-done.6.refs_1_
  33.8 1.2 %collective-permute-start.11 = (bf16[1920,128]{1,0:T(8,128)(2,1)S(1)}, bf16[1920,128]{1,0:T(8,128)(2,1)S(1)}, u32[]{:S(2)}, u32[]{:S(2)}) collective-permute-start(bf16[1920,128]{1,0:T(8,128)(2,1)S(1)} %collective-permute-done.6.refs_1_), channel_id=1, source_target_pairs={{0,1},{1,0},{2,3},{3,2},{4,5},{5,4},{6,7},{7,6},{8,9},{9,8},{10,11... | collective-permute-start | bytes 1474568 | tf_op jit(solution)/shard_map/ppermute | solution.py:33
  35.0 0.2 collective-permute-start.9
  35.2 1.3 %collective-permute-done.11.refs_3_ = bf16[1920,128]{1,0:T(8,128)(2,1)S(1)} collective-permute-done((bf16[1920,128]{1,0:T(8,128)(2,1)S(1)}, bf16[1920,128]{1,0:T(8,128)(2,1)S(1)}, u32[]{:S(2)}, u32[]{:S(2)}) %collective-permute-start.11) | collective-permute-done | bytes 491552 | tf_op jit(solution)/shard_map/ppermute | solution.py:33
  36.5 4.3 %fold.1.refs_1_ = bf16[192,960]{1,0:T(8,128)(2,1)S(1)} custom-call(bf16[1920,128]{1,0:T(8,128)(2,1)S(1)} %embed_four.1.refs_0_, bf16[1920,128]{1,0:T(8,128)(2,1)S(1)} %collective-permute-done.6.refs_1_, bf16[1920,128]{1,0:T(8,128)(2,1)S(1)} %collective-permute-done.10.refs_2_, bf16[1920,128]{1,0:T(8,128)(2,1)S(1)} %collective-permute-done.11.refs_3_, ...), custom_call_target="tpu_custom_call" | custom-call | flops 4000000000 | bytes 12000000 | tf_op jit(solution)/shard_map/fold/pallas_call | solution.py:223
  40.8 0.0 copy-start
  40.8 0.7 collective-permute-done.9.refs_1_
  41.5 0.1 collective-permute-start.12
  41.6 1.6 %collective-permute-start.13 = (bf16[128,1536]{1,0:T(8,128)(2,1)S(1)}, bf16[128,1536]{1,0:T(8,128)(2,1)S(1)}, u32[]{:S(2)}, u32[]{:S(2)}) collective-permute-start(bf16[128,1536]{1,0:T(8,128)(2,1)S(1)} %patch_pair.1.refs_0_), channel_id=1, source_target_pairs={{0,6},{1,7},{2,4},{3,5},{4,2},{5,3},{6,0},{7,1},{8,14},{9,15},{10,... | collective-permute-start | bytes 1179656 | tf_op jit(solution)/shard_map/ppermute | solution.py:33
  43.2 0.0 collective-permute-start.14
  43.2 1.8 %collective-permute-start.15 = (bf16[192,960]{1,0:T(8,128)(2,1)S(1)}, bf16[192,960]{1,0:T(8,128)(2,1)S(1)}, u32[]{:S(2)}, u32[]{:S(2)}) collective-permute-start(bf16[192,960]{1,0:T(8,128)(2,1)S(1)} %fold.1.refs_1_), channel_id=1, source_target_pairs={{0,48},{16,32},{32,16},{48,0},{64,112},{80,96},{96,80},{112,64},{1... | collective-permute-start | bytes 1105928 | tf_op jit(solution)/shard_map/ppermute | solution.py:37
  45.0 1.6 %collective-permute-start.16 = (bf16[192,960]{1,0:T(8,128)(2,1)S(1)}, bf16[192,960]{1,0:T(8,128)(2,1)S(1)}, u32[]{:S(2)}, u32[]{:S(2)}) collective-permute-start(bf16[192,960]{1,0:T(8,128)(2,1)S(1)} %fold.1.refs_1_), channel_id=1, source_target_pairs={{0,64},{16,80},{32,96},{48,112},{64,0},{80,16},{96,32},{112,48},{1... | collective-permute-start | bytes 1105928 | tf_op jit(solution)/shard_map/ppermute | solution.py:37
  46.5 6.2 %collective-permute-done.14.refs_0_.refs_2_ = bf16[192,960]{1,0:T(8,128)(2,1)S(1)} collective-permute-done((bf16[192,960]{1,0:T(8,128)(2,1)S(1)}, bf16[192,960]{1,0:T(8,128)(2,1)S(1)}, u32[]{:S(2)}, u32[]{:S(2)}) %collective-permute-start.14) | collective-permute-done | bytes 368672 | tf_op jit(solution)/shard_map/ppermute | solution.py:37
  52.8 1.2 %collective-permute-done.15.refs_2_.refs_3_ = bf16[192,960]{1,0:T(8,128)(2,1)S(1)} collective-permute-done((bf16[192,960]{1,0:T(8,128)(2,1)S(1)}, bf16[192,960]{1,0:T(8,128)(2,1)S(1)}, u32[]{:S(2)}, u32[]{:S(2)}) %collective-permute-start.15) | collective-permute-done | bytes 368672 | tf_op jit(solution)/shard_map/ppermute | solution.py:37
  54.0 1.5 %collective-permute-done.16.refs_1_.refs_4_ = bf16[192,960]{1,0:T(8,128)(2,1)S(1)} collective-permute-done((bf16[192,960]{1,0:T(8,128)(2,1)S(1)}, bf16[192,960]{1,0:T(8,128)(2,1)S(1)}, u32[]{:S(2)}, u32[]{:S(2)}) %collective-permute-start.16) | collective-permute-done | bytes 368672 | tf_op jit(solution)/shard_map/ppermute | solution.py:37
  55.5 0.1 patch_most.1.refs_0_
  55.6 2.6 %collective-permute-start.19 = (bf16[384,1536]{1,0:T(8,128)(2,1)S(1)}, bf16[384,1536]{1,0:T(8,128)(2,1)S(1)}, u32[]{:S(2)}, u32[]{:S(2)}) collective-permute-start(bf16[384,1536]{1,0:T(8,128)(2,1)S(1)} %patch_most.1.refs_0_), channel_id=1, source_target_pairs={{0,1},{1,0},{2,3},{3,2},{4,5},{5,4},{6,7},{7,6},{8,9},{9,8},{10,11... | collective-permute-start | bytes 3538952 | tf_op jit(solution)/shard_map/ppermute | solution.py:33
  58.2 1.2 %collective-permute-start.17 = (bf16[64,1536]{1,0:T(8,128)(2,1)S(1)}, bf16[64,1536]{1,0:T(8,128)(2,1)S(1)}, u32[]{:S(2)}, u32[]{:S(2)}) collective-permute-start(bf16[64,1536]{1,0:T(8,128)(2,1)S(1)} %get-tuple-element.42), channel_id=1, source_target_pairs={{0,6},{1,7},{2,4},{3,5},{4,2},{5,3},{6,0},{7,1},{8,14},{9,15},{10,... | collective-permute-start | bytes 589832 | tf_op jit(solution)/shard_map/ppermute | solution.py:33
  59.4 0.2 collective-permute-start.18
  59.6 0.1 fold_parts.1
  59.6 1.1 %collective-permute-start.25 = (bf16[288,960]{1,0:T(8,128)(2,1)S(1)}, bf16[288,960]{1,0:T(8,128)(2,1)S(1)}, u32[]{:S(2)}, u32[]{:S(2)}) collective-permute-start(bf16[288,960]{1,0:T(8,128)(2,1)S(1)} %get-tuple-element.49), channel_id=1, source_target_pairs={{0,48},{16,32},{32,16},{48,0},{64,112},{80,96},{96,80},{112,64},{1... | collective-permute-start | bytes 1658888 | tf_op jit(solution)/shard_map/ppermute | solution.py:37
  60.7 0.3 collective-permute-start.26
  61.0 5.1 %collective-permute-done.17.refs_1_ = bf16[64,1536]{1,0:T(8,128)(2,1)S(1)} collective-permute-done((bf16[64,1536]{1,0:T(8,128)(2,1)S(1)}, bf16[64,1536]{1,0:T(8,128)(2,1)S(1)}, u32[]{:S(2)}, u32[]{:S(2)}) %collective-permute-start.17) | collective-permute-done | bytes 196640 | tf_op jit(solution)/shard_map/ppermute | solution.py:33
  66.0 0.8 collective-permute-start.20
  66.8 0.0 collective-permute-done.18.refs_2_
  66.8 0.0 collective-permute-start.21
  66.8 1.1 %collective-permute-done.20.refs_4_ = bf16[64,1536]{1,0:T(8,128)(2,1)S(1)} collective-permute-done((bf16[64,1536]{1,0:T(8,128)(2,1)S(1)}, bf16[64,1536]{1,0:T(8,128)(2,1)S(1)}, u32[]{:S(2)}, u32[]{:S(2)}) %collective-permute-start.20) | collective-permute-done | bytes 196640 | tf_op jit(solution)/shard_map/ppermute | solution.py:33
  67.9 0.4 collective-permute-done.21.refs_5_
  68.3 0.0 collective-permute-done.19.refs_3_
  68.3 1.6 %moments.1 = (f32[8,256]{1,0:T(8,128)S(1)}, bf16[16,64,1536]{2,1,0:T(8,128)(2,1)S(1)}) custom-call(bf16[384,1536]{1,0:T(8,128)(2,1)S(1)} %patch_most.1.refs_0_, bf16[64,1536]{1,0:T(8,128)(2,1)S(1)} %collective-permute-done.17.refs_1_, bf16[64,1536]{1,0:T(8,128)(2,1)S(1)} %collective-permute-done.18.refs_2_, ...), custom_call_target="tpu_custom_call" | custom-call | flops 2000000000 | bytes 5000000 | tf_op jit(solution)/shard_map/moments/pallas_call | solution.py:255
  69.8 1.2 %collective-permute-start.22 = (f32[8,256]{1,0:T(8,128)S(1)}, f32[8,256]{1,0:T(8,128)S(1)}, u32[]{:S(2)}, u32[]{:S(2)}) collective-permute-start(f32[8,256]{1,0:T(8,128)S(1)} %get-tuple-element.45.refs_0_), channel_id=1, source_target_pairs={{0,8},{1,9},{2,10},{3,11},{4,12},{5,13},{6,14},{7,15},{8,0},{9,1},... | collective-permute-start | bytes 24584 | tf_op jit(solution)/shard_map/ppermute | solution.py:33
  71.0 1.7 %collective-permute-done.22.refs_1_ = f32[8,256]{1,0:T(8,128)S(1)} collective-permute-done((f32[8,256]{1,0:T(8,128)S(1)}, f32[8,256]{1,0:T(8,128)S(1)}, u32[]{:S(2)}, u32[]{:S(2)}) %collective-permute-start.22) | collective-permute-done | bytes 8224 | tf_op jit(solution)/shard_map/ppermute | solution.py:33
  72.7 0.1 collective-permute-start.23
  72.8 2.4 %collective-permute-done.25.refs_5_.refs_0_ = bf16[288,960]{1,0:T(8,128)(2,1)S(1)} collective-permute-done((bf16[288,960]{1,0:T(8,128)(2,1)S(1)}, bf16[288,960]{1,0:T(8,128)(2,1)S(1)}, u32[]{:S(2)}, u32[]{:S(2)}) %collective-permute-start.25) | collective-permute-done | bytes 552992 | tf_op jit(solution)/shard_map/ppermute | solution.py:37
  75.2 0.0 collective-permute-done.26.refs_6_.refs_1_
  75.3 0.1 collective-permute-start.27
  75.4 1.4 %collective-permute-start.28 = (bf16[96,960]{1,0:T(8,128)(2,1)S(1)}, bf16[96,960]{1,0:T(8,128)(2,1)S(1)}, u32[]{:S(2)}, u32[]{:S(2)}) collective-permute-start(bf16[96,960]{1,0:T(8,128)(2,1)S(1)} %get-tuple-element.53), channel_id=1, source_target_pairs={{0,48},{16,32},{32,16},{48,0},{64,112},{80,96},{96,80},{112,64},{1... | collective-permute-start | bytes 552968 | tf_op jit(solution)/shard_map/ppermute | solution.py:37
  76.7 0.0 collective-permute-done.23.refs_1_
  76.8 1.7 %collective-permute-start.24 = (f32[8,256]{1,0:T(8,128)S(1)}, f32[8,256]{1,0:T(8,128)S(1)}, u32[]{:S(2)}, u32[]{:S(2)}) collective-permute-start(f32[8,256]{1,0:T(8,128)S(1)} %merge.5.refs_0_), channel_id=1, source_target_pairs={{0,6},{1,7},{2,4},{3,5},{4,2},{5,3},{6,0},{7,1},{8,14},{9,15},{10,... | collective-permute-start | bytes 24584 | tf_op jit(solution)/shard_map/ppermute | solution.py:33
  78.5 3.6 %project_most.1.total = f32[1024,960]{1,0:T(8,128)S(1)} custom-call(bf16[16,64,1536]{2,1,0:T(8,128)(2,1)S(1)} %get-tuple-element.44.refs_0_.tokens, bf16[192,960]{1,0:T(8,128)(2,1)S(1)} %fold.1.refs_1_, bf16[192,960]{1,0:T(8,128)(2,1)S(1)} %collective-permute-done.14.refs_0_.refs_2_, bf16[192,960]{1,0:T(8,128)(2,1)S(1)} %collective-permute-done.15.refs_2_.refs_3_, ...), custom_call_target="tpu_custom_call" | custom-call | flops 4000000000 | bytes 8000000 | tf_op jit(solution)/shard_map/project_most/pallas_call | solution.py:301
  82.1 0.0 collective-permute-done.24.refs_1_
  82.2 2.4 %collective-permute-start.29 = (f32[8,256]{1,0:T(8,128)S(1)}, f32[8,256]{1,0:T(8,128)S(1)}, u32[]{:S(2)}, u32[]{:S(2)}) collective-permute-start(f32[8,256]{1,0:T(8,128)S(1)} %merge.6.refs_0_), channel_id=1, source_target_pairs={{0,1},{1,0},{2,3},{3,2},{4,5},{5,4},{6,7},{7,6},{8,9},{9,8},{10,11... | collective-permute-start | bytes 24584 | tf_op jit(solution)/shard_map/ppermute | solution.py:33
  84.5 0.8 collective-permute-done.29.refs_1_
  85.4 0.0 collective-permute-done.27.low
  85.4 0.0 collective-permute-done.28.high
  85.4 2.2 %project_last.1 = bf16[4,16,16,960]{3,2,1,0:T(8,128)(2,1)} custom-call(bf16[16,64,1536]{2,1,0:T(8,128)(2,1)S(1)} %get-tuple-element.44.refs_0_.tokens, f32[1024,960]{1,0:T(8,128)S(1)} %project_most.1.total, bf16[96,960]{1,0:T(8,128)(2,1)S(1)} %collective-permute-done.27.low, bf16[96,960]{1,0:T(8,128)(2,1)S(1)} %collective-permute-done.28.high, ...), custom_call_target="tpu_custom_call" | custom-call | flops 2000000000 | bytes 8000000 | tf_op jit(solution)/shard_map/project_last/pallas_call | solution.py:338
  (21 shorter events, 0.2 us)
Async XLA Ops:
  0.0 10.7 %collective-permute-start.3 = (bf16[4,2,32,192]{3,2,1,0:T(8,128)(2,1)}, bf16[4,2,32,192]{3,2,1,0:T(8,128)(2,1)S(1)}, u32[]{:S(2)}, u32[]{:S(2)}) collective-permute-start(bf16[4,2,32,192]{3,2,1,0:T(8,128)(2,1)} %video.1), channel_id=1, source_target_pairs={{0,16},{16,32},{32,48},{48,64},{64,80},{80,96},{96,112},{112,0},{1... | collective-permute-start | bytes 294920 | tf_op jit(solution)/shard_map/ppermute | solution.py:37
  3.2 17.9 %collective-permute-start = (bf16[480,128]{1,0:T(8,128)(2,1)S(1)}, bf16[480,128]{1,0:T(8,128)(2,1)S(1)}, u32[]{:S(2)}, u32[]{:S(2)}) collective-permute-start(bf16[480,128]{1,0:T(8,128)(2,1)S(1)} %embed_slice.1.refs_0_), channel_id=1, source_target_pairs={{0,2},{1,3},{2,0},{3,1},{4,6},{5,7},{6,4},{7,5},{8,10},{9,11},{10,... | collective-permute-start | bytes 368648 | tf_op jit(solution)/shard_map/ppermute | solution.py:33
  4.9 16.2 %collective-permute-start.1 = (bf16[480,128]{1,0:T(8,128)(2,1)S(1)}, bf16[480,128]{1,0:T(8,128)(2,1)S(1)}, u32[]{:S(2)}, u32[]{:S(2)}) collective-permute-start(bf16[480,128]{1,0:T(8,128)(2,1)S(1)} %embed_slice.1.refs_0_), channel_id=1, source_target_pairs={{0,6},{1,7},{2,4},{3,5},{4,2},{5,3},{6,0},{7,1},{8,14},{9,15},{10,... | collective-permute-start | bytes 368648 | tf_op jit(solution)/shard_map/ppermute | solution.py:33
  7.1 14.0 %collective-permute-start.2 = (bf16[480,128]{1,0:T(8,128)(2,1)S(1)}, bf16[480,128]{1,0:T(8,128)(2,1)S(1)}, u32[]{:S(2)}, u32[]{:S(2)}) collective-permute-start(bf16[480,128]{1,0:T(8,128)(2,1)S(1)} %embed_slice.1.refs_0_), channel_id=1, source_target_pairs={{0,4},{1,5},{2,6},{3,7},{4,0},{5,1},{6,2},{7,3},{8,12},{9,13},{10,... | collective-permute-start | bytes 368648 | tf_op jit(solution)/shard_map/ppermute | solution.py:33
  8.2 9.3 %collective-permute-start.4 = (bf16[4,2,32,192]{3,2,1,0:T(8,128)(2,1)}, bf16[4,2,32,192]{3,2,1,0:T(8,128)(2,1)S(1)}, u32[]{:S(2)}, u32[]{:S(2)}) collective-permute-start(bf16[4,2,32,192]{3,2,1,0:T(8,128)(2,1)} %video.1), channel_id=1, source_target_pairs={{0,31},{1,18},{2,17},{3,20},{4,19},{5,22},{6,21},{7,24},{8,23},{9,... | collective-permute-start | bytes 294920 | tf_op jit(solution)/shard_map/ppermute | solution.py:405
  10.7 10.3 %collective-permute-start.5 = (bf16[4,2,32,192]{3,2,1,0:T(8,128)(2,1)}, bf16[4,2,32,192]{3,2,1,0:T(8,128)(2,1)S(1)}, u32[]{:S(2)}, u32[]{:S(2)}) collective-permute-start(bf16[4,2,32,192]{3,2,1,0:T(8,128)(2,1)} %video.1), channel_id=1, source_target_pairs={{0,15},{1,2},{2,1},{3,4},{4,3},{5,6},{6,5},{7,8},{8,7},{9,10},{10,... | collective-permute-start | bytes 294920 | tf_op jit(solution)/shard_map/ppermute | solution.py:33
  17.4 4.8 %collective-permute-start.7 = (bf16[4,2,32,192]{3,2,1,0:T(8,128)(2,1)}, bf16[4,2,32,192]{3,2,1,0:T(8,128)(2,1)S(1)}, u32[]{:S(2)}, u32[]{:S(2)}) collective-permute-start(bf16[4,2,32,192]{3,2,1,0:T(8,128)(2,1)} %video.1), channel_id=1, source_target_pairs={{0,1},{1,0},{2,3},{3,2},{4,5},{5,4},{6,7},{7,6},{8,9},{9,8},{10,11... | collective-permute-start | bytes 294920 | tf_op jit(solution)/shard_map/ppermute | solution.py:33
  21.1 1.4 %collective-permute-start.8 = (bf16[4,2,32,192]{3,2,1,0:T(8,128)(2,1)S(1)}, bf16[4,2,32,192]{3,2,1,0:T(8,128)(2,1)S(1)}, u32[]{:S(2)}, u32[]{:S(2)}) collective-permute-start(bf16[4,2,32,192]{3,2,1,0:T(8,128)(2,1)S(1)} %collective-permute-done.3.back), channel_id=1, source_target_pairs={{0,1},{1,0},{2,3},{3,2},{4,5},{5,4},{6,7},{7,6},{8,9},{9,8},{10,11... | collective-permute-start | bytes 294920 | tf_op jit(solution)/shard_map/ppermute | solution.py:33
  21.2 15.3 %slice-start = ((s8[9830400]{0:T(1024)(128)(4,1)}), s8[4194304]{0:T(1024)(128)(4,1)S(1)}, s32[]{:S(2)}) async-start(s8[9830400]{0:T(1024)(128)(4,1)} %bitcast.6), calls=%async_computation | async-start | bytes 8388608
  21.3 12.5 %collective-permute-start.6 = (bf16[1920,128]{1,0:T(8,128)(2,1)S(1)}, bf16[1920,128]{1,0:T(8,128)(2,1)S(1)}, u32[]{:S(2)}, u32[]{:S(2)}) collective-permute-start(bf16[1920,128]{1,0:T(8,128)(2,1)S(1)} %embed_four.1.refs_0_), channel_id=1, source_target_pairs={{0,8},{1,9},{2,10},{3,11},{4,12},{5,13},{6,14},{7,15},{8,0},{9,1},... | collective-permute-start | bytes 1474568 | tf_op jit(solution)/shard_map/ppermute | solution.py:33
  21.3 13.8 %collective-permute-start.10 = (bf16[1920,128]{1,0:T(8,128)(2,1)S(1)}, bf16[1920,128]{1,0:T(8,128)(2,1)S(1)}, u32[]{:S(2)}, u32[]{:S(2)}) collective-permute-start(bf16[1920,128]{1,0:T(8,128)(2,1)S(1)} %embed_four.1.refs_0_), channel_id=1, source_target_pairs={{0,1},{1,0},{2,3},{3,2},{4,5},{5,4},{6,7},{7,6},{8,9},{9,8},{10,11... | collective-permute-start | bytes 1474568 | tf_op jit(solution)/shard_map/ppermute | solution.py:33
  22.5 13.9 %slice-start.1 = ((s8[9830400]{0:T(1024)(128)(4,1)}), s8[4194304]{0:T(1024)(128)(4,1)S(1)}, s32[]{:S(2)}) async-start(s8[9830400]{0:T(1024)(128)(4,1)} %bitcast.6), calls=%async_computation.1 | async-start | bytes 8388608
  22.5 13.9 %slice-start.2 = ((s8[9830400]{0:T(1024)(128)(4,1)}), s8[1441792]{0:T(1024)(128)(4,1)S(1)}, s32[]{:S(2)}) async-start(s8[9830400]{0:T(1024)(128)(4,1)} %bitcast.6), calls=%async_computation.2 | async-start | bytes 2883584
  33.8 2.7 %collective-permute-start.11 = (bf16[1920,128]{1,0:T(8,128)(2,1)S(1)}, bf16[1920,128]{1,0:T(8,128)(2,1)S(1)}, u32[]{:S(2)}, u32[]{:S(2)}) collective-permute-start(bf16[1920,128]{1,0:T(8,128)(2,1)S(1)} %collective-permute-done.6.refs_1_), channel_id=1, source_target_pairs={{0,1},{1,0},{2,3},{3,2},{4,5},{5,4},{6,7},{7,6},{8,9},{9,8},{10,11... | collective-permute-start | bytes 1474568 | tf_op jit(solution)/shard_map/ppermute | solution.py:33
  35.0 6.5 %collective-permute-start.9 = (bf16[64,1536]{1,0:T(8,128)(2,1)S(1)}, bf16[64,1536]{1,0:T(8,128)(2,1)S(1)}, u32[]{:S(2)}, u32[]{:S(2)}) collective-permute-start(bf16[64,1536]{1,0:T(8,128)(2,1)S(1)} %convolutions.1.refs_0_), channel_id=1, source_target_pairs={{0,8},{1,9},{2,10},{3,11},{4,12},{5,13},{6,14},{7,15},{8,0},{9,1},... | collective-permute-start | bytes 589832 | tf_op jit(solution)/shard_map/ppermute | solution.py:33
  40.8 27.5 %copy-start = (bf16[1536,320]{0,1:T(8,128)(2,1)S(1)}, bf16[1536,320]{0,1:T(8,128)(2,1)}, u32[]{:S(2)}) copy-start(bf16[1536,320]{0,1:T(8,128)(2,1)} %param.10) | copy-start | bytes 2949124
  41.5 13.9 %collective-permute-start.12 = (bf16[128,1536]{1,0:T(8,128)(2,1)S(1)}, bf16[128,1536]{1,0:T(8,128)(2,1)S(1)}, u32[]{:S(2)}, u32[]{:S(2)}) collective-permute-start(bf16[128,1536]{1,0:T(8,128)(2,1)S(1)} %patch_pair.1.refs_0_), channel_id=1, source_target_pairs={{0,2},{1,3},{2,0},{3,1},{4,6},{5,7},{6,4},{7,5},{8,10},{9,11},{10,... | collective-permute-start | bytes 1179656 | tf_op jit(solution)/shard_map/ppermute | solution.py:33
  41.6 13.8 %collective-permute-start.13 = (bf16[128,1536]{1,0:T(8,128)(2,1)S(1)}, bf16[128,1536]{1,0:T(8,128)(2,1)S(1)}, u32[]{:S(2)}, u32[]{:S(2)}) collective-permute-start(bf16[128,1536]{1,0:T(8,128)(2,1)S(1)} %patch_pair.1.refs_0_), channel_id=1, source_target_pairs={{0,6},{1,7},{2,4},{3,5},{4,2},{5,3},{6,0},{7,1},{8,14},{9,15},{10,... | collective-permute-start | bytes 1179656 | tf_op jit(solution)/shard_map/ppermute | solution.py:33
  43.2 9.5 %collective-permute-start.14 = (bf16[192,960]{1,0:T(8,128)(2,1)S(1)}, bf16[192,960]{1,0:T(8,128)(2,1)S(1)}, u32[]{:S(2)}, u32[]{:S(2)}) collective-permute-start(bf16[192,960]{1,0:T(8,128)(2,1)S(1)} %fold.1.refs_1_), channel_id=1, source_target_pairs={{0,16},{16,0},{32,48},{48,32},{64,80},{80,64},{96,112},{112,96},{1... | collective-permute-start | bytes 1105928 | tf_op jit(solution)/shard_map/ppermute | solution.py:37
  43.2 10.8 %collective-permute-start.15 = (bf16[192,960]{1,0:T(8,128)(2,1)S(1)}, bf16[192,960]{1,0:T(8,128)(2,1)S(1)}, u32[]{:S(2)}, u32[]{:S(2)}) collective-permute-start(bf16[192,960]{1,0:T(8,128)(2,1)S(1)} %fold.1.refs_1_), channel_id=1, source_target_pairs={{0,48},{16,32},{32,16},{48,0},{64,112},{80,96},{96,80},{112,64},{1... | collective-permute-start | bytes 1105928 | tf_op jit(solution)/shard_map/ppermute | solution.py:37
  45.0 10.5 %collective-permute-start.16 = (bf16[192,960]{1,0:T(8,128)(2,1)S(1)}, bf16[192,960]{1,0:T(8,128)(2,1)S(1)}, u32[]{:S(2)}, u32[]{:S(2)}) collective-permute-start(bf16[192,960]{1,0:T(8,128)(2,1)S(1)} %fold.1.refs_1_), channel_id=1, source_target_pairs={{0,64},{16,80},{32,96},{48,112},{64,0},{80,16},{96,32},{112,48},{1... | collective-permute-start | bytes 1105928 | tf_op jit(solution)/shard_map/ppermute | solution.py:37
  55.6 12.7 %collective-permute-start.19 = (bf16[384,1536]{1,0:T(8,128)(2,1)S(1)}, bf16[384,1536]{1,0:T(8,128)(2,1)S(1)}, u32[]{:S(2)}, u32[]{:S(2)}) collective-permute-start(bf16[384,1536]{1,0:T(8,128)(2,1)S(1)} %patch_most.1.refs_0_), channel_id=1, source_target_pairs={{0,1},{1,0},{2,3},{3,2},{4,5},{5,4},{6,7},{7,6},{8,9},{9,8},{10,11... | collective-permute-start | bytes 3538952 | tf_op jit(solution)/shard_map/ppermute | solution.py:33
  58.2 7.8 %collective-permute-start.17 = (bf16[64,1536]{1,0:T(8,128)(2,1)S(1)}, bf16[64,1536]{1,0:T(8,128)(2,1)S(1)}, u32[]{:S(2)}, u32[]{:S(2)}) collective-permute-start(bf16[64,1536]{1,0:T(8,128)(2,1)S(1)} %get-tuple-element.42), channel_id=1, source_target_pairs={{0,6},{1,7},{2,4},{3,5},{4,2},{5,3},{6,0},{7,1},{8,14},{9,15},{10,... | collective-permute-start | bytes 589832 | tf_op jit(solution)/shard_map/ppermute | solution.py:33
  59.4 7.4 %collective-permute-start.18 = (bf16[64,1536]{1,0:T(8,128)(2,1)S(1)}, bf16[64,1536]{1,0:T(8,128)(2,1)S(1)}, u32[]{:S(2)}, u32[]{:S(2)}) collective-permute-start(bf16[64,1536]{1,0:T(8,128)(2,1)S(1)} %get-tuple-element.43), channel_id=1, source_target_pairs={{0,2},{1,3},{2,0},{3,1},{4,6},{5,7},{6,4},{7,5},{8,10},{9,11},{10,... | collective-permute-start | bytes 589832 | tf_op jit(solution)/shard_map/ppermute | solution.py:33
  59.6 15.6 %collective-permute-start.25 = (bf16[288,960]{1,0:T(8,128)(2,1)S(1)}, bf16[288,960]{1,0:T(8,128)(2,1)S(1)}, u32[]{:S(2)}, u32[]{:S(2)}) collective-permute-start(bf16[288,960]{1,0:T(8,128)(2,1)S(1)} %get-tuple-element.49), channel_id=1, source_target_pairs={{0,48},{16,32},{32,16},{48,0},{64,112},{80,96},{96,80},{112,64},{1... | collective-permute-start | bytes 1658888 | tf_op jit(solution)/shard_map/ppermute | solution.py:37
  60.7 14.5 %collective-permute-start.26 = (bf16[288,960]{1,0:T(8,128)(2,1)S(1)}, bf16[288,960]{1,0:T(8,128)(2,1)S(1)}, u32[]{:S(2)}, u32[]{:S(2)}) collective-permute-start(bf16[288,960]{1,0:T(8,128)(2,1)S(1)} %get-tuple-element.50), channel_id=1, source_target_pairs={{0,16},{16,0},{32,48},{48,32},{64,80},{80,64},{96,112},{112,96},{1... | collective-permute-start | bytes 1658888 | tf_op jit(solution)/shard_map/ppermute | solution.py:37
  66.0 1.9 %collective-permute-start.20 = (bf16[64,1536]{1,0:T(8,128)(2,1)S(1)}, bf16[64,1536]{1,0:T(8,128)(2,1)S(1)}, u32[]{:S(2)}, u32[]{:S(2)}) collective-permute-start(bf16[64,1536]{1,0:T(8,128)(2,1)S(1)} %collective-permute-done.17.refs_1_), channel_id=1, source_target_pairs={{0,1},{1,0},{2,3},{3,2},{4,5},{5,4},{6,7},{7,6},{8,9},{9,8},{10,11... | collective-permute-start | bytes 589832 | tf_op jit(solution)/shard_map/ppermute | solution.py:33
  66.8 1.4 %collective-permute-start.21 = (bf16[64,1536]{1,0:T(8,128)(2,1)S(1)}, bf16[64,1536]{1,0:T(8,128)(2,1)S(1)}, u32[]{:S(2)}, u32[]{:S(2)}) collective-permute-start(bf16[64,1536]{1,0:T(8,128)(2,1)S(1)} %collective-permute-done.18.refs_2_), channel_id=1, source_target_pairs={{0,1},{1,0},{2,3},{3,2},{4,5},{5,4},{6,7},{7,6},{8,9},{9,8},{10,11... | collective-permute-start | bytes 589832 | tf_op jit(solution)/shard_map/ppermute | solution.py:33
  69.8 2.9 %collective-permute-start.22 = (f32[8,256]{1,0:T(8,128)S(1)}, f32[8,256]{1,0:T(8,128)S(1)}, u32[]{:S(2)}, u32[]{:S(2)}) collective-permute-start(f32[8,256]{1,0:T(8,128)S(1)} %get-tuple-element.45.refs_0_), channel_id=1, source_target_pairs={{0,8},{1,9},{2,10},{3,11},{4,12},{5,13},{6,14},{7,15},{8,0},{9,1},... | collective-permute-start | bytes 24584 | tf_op jit(solution)/shard_map/ppermute | solution.py:33
  72.7 4.0 %collective-permute-start.23 = (f32[8,256]{1,0:T(8,128)S(1)}, f32[8,256]{1,0:T(8,128)S(1)}, u32[]{:S(2)}, u32[]{:S(2)}) collective-permute-start(f32[8,256]{1,0:T(8,128)S(1)} %merge.4.refs_0_), channel_id=1, source_target_pairs={{0,2},{1,3},{2,0},{3,1},{4,6},{5,7},{6,4},{7,5},{8,10},{9,11},{10,... | collective-permute-start | bytes 24584 | tf_op jit(solution)/shard_map/ppermute | solution.py:33
  75.3 10.1 %collective-permute-start.27 = (bf16[96,960]{1,0:T(8,128)(2,1)S(1)}, bf16[96,960]{1,0:T(8,128)(2,1)S(1)}, u32[]{:S(2)}, u32[]{:S(2)}) collective-permute-start(bf16[96,960]{1,0:T(8,128)(2,1)S(1)} %get-tuple-element.52), channel_id=1, source_target_pairs={{0,16},{16,0},{32,48},{48,32},{64,80},{80,64},{96,112},{112,96},{1... | collective-permute-start | bytes 552968 | tf_op jit(solution)/shard_map/ppermute | solution.py:37
  75.4 10.0 %collective-permute-start.28 = (bf16[96,960]{1,0:T(8,128)(2,1)S(1)}, bf16[96,960]{1,0:T(8,128)(2,1)S(1)}, u32[]{:S(2)}, u32[]{:S(2)}) collective-permute-start(bf16[96,960]{1,0:T(8,128)(2,1)S(1)} %get-tuple-element.53), channel_id=1, source_target_pairs={{0,48},{16,32},{32,16},{48,0},{64,112},{80,96},{96,80},{112,64},{1... | collective-permute-start | bytes 552968 | tf_op jit(solution)/shard_map/ppermute | solution.py:37
  76.8 5.4 %collective-permute-start.24 = (f32[8,256]{1,0:T(8,128)S(1)}, f32[8,256]{1,0:T(8,128)S(1)}, u32[]{:S(2)}, u32[]{:S(2)}) collective-permute-start(f32[8,256]{1,0:T(8,128)S(1)} %merge.5.refs_0_), channel_id=1, source_target_pairs={{0,6},{1,7},{2,4},{3,5},{4,2},{5,3},{6,0},{7,1},{8,14},{9,15},{10,... | collective-permute-start | bytes 24584 | tf_op jit(solution)/shard_map/ppermute | solution.py:33
  82.2 3.2 %collective-permute-start.29 = (f32[8,256]{1,0:T(8,128)S(1)}, f32[8,256]{1,0:T(8,128)S(1)}, u32[]{:S(2)}, u32[]{:S(2)}) collective-permute-start(f32[8,256]{1,0:T(8,128)S(1)} %merge.6.refs_0_), channel_id=1, source_target_pairs={{0,1},{1,0},{2,3},{3,2},{4,5},{5,4},{6,7},{7,6},{8,9},{9,8},{10,11... | collective-permute-start | bytes 24584 | tf_op jit(solution)/shard_map/ppermute | solution.py:33
